TPU v7x, 256 devices: a whole 4x4x8 slice. The times are simulated.
256 devices in a mesh: gx: 8 (over z), gy: 32 (over x, y, core).
Axes of the slice: x: 4, y: 4, z: 8, core: 2. Of those that a mesh axis runs over, the one named last changes fastest.
Arguments:
- right_side: float32 [128, 256, 128], P('gx', 'gy'), may hold values from -6 to 6
- alpha: float32 [128, 256, 128], P('gx', 'gy'), may hold values from 0.1 to 40
- beta_x: float32 [128, 256, 128], P('gx', 'gy'), may hold values from 0.125 to 8
- beta_y: float32 [128, 256, 128], P('gx', 'gy'), may hold values from 0.125 to 8
- beta_z: float32 [128, 256, 128], P('gx', 'gy'), may hold values from 0.125 to 8
Outputs:
- correction: float32 [128, 256, 128], P('gx', 'gy')
All inputs are finite; a program needn't handle non-finite values.
Results may differ from a plain program's by a relative error of at most 0.0001.
Values sent between devices are 32-bit elements; how exact they have to be, the bound alone decides.
A program may use at most 320 MiB of HBM per device.

v0:
```python
import jax
import jax.numpy as jnp
from jax import lax
from jax.sharding import PartitionSpec as P

LEVELS = 5
SWEEPS = 4
COARSE_SWEEPS = 12


SHIFT = 0.002
LOW = 0.25
HIGH = 2.0
COARSE_LOW = 0.1


def padded_2(array, sides, width):
    for axis, dim in sides:
        count, length = (lax.axis_size(axis), array.shape[dim])
        up = [(i, (i + 1) % count) for i in range(count - 1)]
        down = [(j, i) for i, j in up]
        last = lax.slice_in_dim(array, length - width, length, axis=dim)
        initial = lax.slice_in_dim(array, 0, width, axis=dim)
        before = lax.ppermute(last, axis, up)
        after = lax.ppermute(initial, axis, down)
        array = jnp.concatenate([before, array, after], axis=dim)
    return array


def passed_along(block, axis, distance):
    devices = range(lax.axis_size(axis))
    route = [(i - distance, i) for i in devices if i - distance in devices]
    return lax.ppermute(block, axis, route)


def chebyshev_table(count, lower, upper):
    theta = (upper + lower) / 2.0
    delta = (upper - lower) / 2.0
    sigma = theta / delta
    rho_prev = 1.0 / sigma
    table = []
    for sweep in range(count):
        if sweep == 0:
            table.append((0.0, 1.0 / theta))
        else:
            rho_next = 1.0 / (2.0 * sigma - rho_prev)
            table.append((rho_next * rho_prev, 2.0 * rho_next / delta))
            rho_prev = rho_next
    return table


def restrict_cells(values):
    size_x, size_y, size_z = values.shape
    return values.reshape(size_x // 2, 2, size_y // 2, 2, size_z // 2, 2).mean(axis=(1, 3, 5))


def prolong(values):
    size_x, size_y, size_z = values.shape
    spread = jnp.broadcast_to(values[:, None, :, None, :, None], (size_x, 2, size_y, 2, size_z, 2))
    return spread.reshape(2 * size_x, 2 * size_y, 2 * size_z)


def restrict_coefs(coeffs):
    alpha, face_x, face_y, face_z = coeffs
    size_x, size_y, size_z = alpha.shape
    new_alpha = restrict_cells(alpha)
    new_x = face_x[0::2].reshape(size_x // 2 + 1, size_y // 2, 2, size_z // 2, 2).mean(axis=(2, 4))
    new_y = (
        face_y[:, 0::2].reshape(size_x // 2, 2, size_y // 2 + 1, size_z // 2, 2).mean(axis=(1, 4))
    )
    new_z = (
        face_z[:, :, 0::2].reshape(size_x // 2, 2, size_y // 2, 2, size_z // 2).mean(axis=(1, 3))
    )
    return (new_alpha, new_x, new_y, new_z)


def prepare(coeffs, level):
    alpha, face_x, face_y, face_z = coeffs
    upper_z = jnp.concatenate([face_z[:, :, 1:], jnp.zeros_like(face_z[:, :, :1])], axis=2)
    scale = 0.25**level
    diagonal = SHIFT * alpha + scale * (
        face_x[:-1] + face_x[1:] + face_y[:, :-1] + face_y[:, 1:] + face_z + upper_z
    )
    return (alpha, face_x, face_y, face_z, upper_z, 1.0 / diagonal, scale)


def operate(padded, coeffs):
    alpha, face_x, face_y, face_z, upper_z, inverse, scale = coeffs
    centre = padded[1:-1, 1:-1]
    flux_x = face_x[:-1] * (centre - padded[:-2, 1:-1]) + face_x[1:] * (centre - padded[2:, 1:-1])
    flux_y = face_y[:, :-1] * (centre - padded[1:-1, :-2]) + face_y[:, 1:] * (
        centre - padded[1:-1, 2:]
    )
    along_z = jnp.pad(centre, ((0, 0), (0, 0), (1, 1)))
    flux_z = face_z * (centre - along_z[:, :, :-2]) + upper_z * (centre - along_z[:, :, 2:])
    return SHIFT * alpha * centre + scale * (flux_x + flux_y + flux_z)


def local_pad(field):
    return jnp.pad(field, ((1, 1), (1, 1), (0, 0)))


def exchange_pad(field):
    return padded_2(field, (("gx", 0), ("gy", 1)), 1)


def smooth(field, source, coeffs, count, lower, upper, padder):
    inverse = coeffs[5]
    update = None
    for sweep, (keep, gain) in enumerate(chebyshev_table(count, lower, upper)):
        if field is None:
            resid = inverse * source
        else:
            resid = inverse * (source - operate(padder(field), coeffs))
        update = gain * resid if sweep == 0 else keep * update + gain * resid
        field = update if field is None else field + update
    return field


def cycle(source, levels):
    return smooth(None, source, levels[0], COARSE_SWEEPS, COARSE_LOW, HIGH, local_pad)


def assemble(piece, count_x, count_y):
    total, size_x, size_y, size_z = piece.shape
    blocks = piece.reshape(count_x, count_y, size_x, size_y, size_z).transpose(0, 2, 1, 3, 4)
    return blocks.reshape(count_x * size_x, count_y * size_y, size_z)


def shards(right_side, alpha, beta_x, beta_y, beta_z):
    count_x = lax.axis_size("gx")
    count_y = lax.axis_size("gy")
    first = LEVELS - 1
    kept = min(first, LEVELS - 2)
    upper_x = passed_along(beta_x[0:1], "gx", -1)
    upper_y = passed_along(beta_y[:, 0:1], "gy", -1)
    raw = [
        (
            alpha,
            jnp.concatenate([beta_x, upper_x], axis=0),
            jnp.concatenate([beta_y, upper_y], axis=1),
            beta_z,
        )
    ]
    for level in range(kept):
        raw.append(restrict_coefs(raw[-1]))
    local_levels = [prepare(raw[level], level) for level in range(first)]
    own_alpha, own_x, own_y, own_z = raw[kept]
    pieces = (
        lax.all_gather(own_alpha[None], ("gx", "gy"), axis=0, tiled=True),
        lax.all_gather(own_x[:-1][None], ("gx", "gy"), axis=0, tiled=True),
        lax.all_gather(own_y[:, :-1][None], ("gx", "gy"), axis=0, tiled=True),
        lax.all_gather(own_z[None], ("gx", "gy"), axis=0, tiled=True),
    )
    whole = [assemble(piece, count_x, count_y) for piece in pieces]
    whole_raw = [
        (
            whole[0],
            jnp.concatenate([whole[1], jnp.zeros_like(whole[1][:1])], axis=0),
            jnp.concatenate([whole[2], jnp.zeros_like(whole[2][:, :1])], axis=1),
            whole[3],
        )
    ]
    level = 3
    whole_raw.append(restrict_coefs(whole_raw[-1]))
    whole_levels = [prepare(whole_raw[4 - kept], 4)]
    source = right_side
    fields = []
    sources = []
    resid = right_side
    for level in range(first):
        field = smooth(None, source, local_levels[level], SWEEPS, LOW, HIGH, exchange_pad)
        resid = source - operate(exchange_pad(field), local_levels[level])
        fields.append(field)
        sources.append(source)
        if level < first - 1:
            source = restrict_cells(resid)
    gathered = lax.all_gather(resid[None], ("gx", "gy"), axis=0, tiled=True)
    coarse_source = assemble(gathered, count_x, count_y)
    coarse_source = restrict_cells(coarse_source)
    correction = prolong(cycle(coarse_source, whole_levels))
    size_x, size_y, size_z = fields[-1].shape
    correction = lax.dynamic_slice(
        correction,
        (lax.axis_index("gx") * size_x, lax.axis_index("gy") * size_y, 0),
        (size_x, size_y, size_z),
    )
    field = correction
    for level in reversed(range(first)):
        field = smooth(
            fields[level] + correction,
            sources[level],
            local_levels[level],
            SWEEPS,
            LOW,
            HIGH,
            exchange_pad,
        )
        if level > 0:
            correction = prolong(field)
    return field


def solution(mesh):
    in_specs = (
        P("gx", "gy", None),
        P("gx", "gy", None),
        P("gx", "gy", None),
        P("gx", "gy", None),
        P("gx", "gy", None),
    )
    out_specs = P("gx", "gy", None)
    return jax.shard_map(shards, mesh=mesh, in_specs=in_specs, out_specs=out_specs, check_vma=False)
```

profile of v0, /device:TPU:1, one launch (start us, length us, event | category | flops | bytes accessed | tf_op | source)
XLA Modules:
  0.0 907.2 jit_solution(1700702483646800496)
XLA Ops:
  0.8 5.1 collective-permute-start.1
  30.1 4.7 collective-permute-start.6
  48.6 4.8 collective-permute-start.10
  63.1 6.4 reshape.164
  81.0 5.1 collective-permute-start.16
  91.2 5.6 reshape.168
  103.6 71.8 %all-gather.7 = f32[256,2,16]{2,1,0:T(2,128)S(1)} all-gather(f32[1,2,16]{2,1,0:T(2,128)S(1)} %get-tuple-element.192), channel_id=5, replica_groups=mesh['gx'=8,'gy'=32] {'gx','gy'}, dimensions={0}, use_global_device_ids=true | all-gather | bytes 32896 | tf_op jit(solution)/shard_map/all_gather | solution.py:153
  214.9 4.1 collective-permute-start.30
  220.2 66.7 %all-gather.6 = f32[256,2,16]{2,1,0:T(2,128)S(1)} all-gather(f32[1,2,16]{2,1,0:T(2,128)S(1)} %slice_bitcast_fusion), channel_id=3, replica_groups=mesh['gx'=8,'gy'=32] {'gx','gy'}, dimensions={0}, use_global_device_ids=true | all-gather | bytes 32896 | tf_op jit(solution)/shard_map/all_gather | solution.py:151
  327.2 4.1 collective-permute-start.42
  357.3 70.8 %all-gather.5 = f32[256,2,16]{2,1,0:T(2,128)S(1)} all-gather(f32[1,2,16]{2,1,0:T(2,128)S(1)} %multiply_bitcast_fusion), channel_id=2, replica_groups=mesh['gx'=8,'gy'=32] {'gx','gy'}, dimensions={0}, use_global_device_ids=true | all-gather | bytes 32896 | tf_op jit(solution)/shard_map/all_gather | solution.py:150
  449.6 63.8 %all-gather.2 = f32[512,1,16]{2,1,0:T(1,128)S(1)} all-gather(f32[2,1,16]{2,1,0:T(1,128)S(1)} %bitcast.366), channel_id=4, replica_groups=mesh['gx'=8,'gy'=32] {'gx','gy'}, dimensions={0}, use_global_device_ids=true | all-gather | bytes 32896 | tf_op jit(solution)/shard_map/all_gather | solution.py:152
  553.2 66.3 %all-gather.4 = f32[512,1,16]{2,1,0:T(1,128)S(1)} all-gather(f32[2,1,16]{2,1,0:T(1,128)S(1)} %bitcast.365), channel_id=6, replica_groups=mesh['gx'=8,'gy'=32] {'gx','gy'}, dimensions={0}, use_global_device_ids=true | all-gather | bytes 32896 | tf_op jit(solution)/shard_map/all_gather | solution.py:178
  711.4 5.4 collective-permute-start.88
  729.0 5.5 collective-permute-start.92
  746.7 5.5 collective-permute-start.96
  764.8 5.5 collective-permute-start.100
  782.6 5.5 collective-permute-start.104
  800.4 5.4 collective-permute-start.108
  818.1 5.4 collective-permute-start.112
  842.6 5.4 collective-permute-start.116
  860.4 5.4 collective-permute-start.120
  878.3 5.4 collective-permute-start.124
  896.1 5.4 collective-permute-start.128
  (486 shorter events, 466.0 us)
Async XLA Ops:
  0.8 10.3 %collective-permute-start.1 = (f32[16,1,128]{2,1,0:T(1,128)S(1)}, f32[16,1,128]{2,1,0:T(1,128)S(1)}, u32[]{:S(2)}, u32[]{:S(2)}) collective-permute-start(f32[16,1,128]{2,1,0:T(1,128)S(1)} %slice.1510), channel_id=1, source_target_pairs={{1,0},{2,1},{3,2},{4,3},{5,4},{6,5},{7,6},{8,7},{9,8},{10,9},{11,1... | collective-permute-start | bytes 24584 | tf_op jit(solution)/shard_map/ppermute | solution.py:33
  30.1 8.0 collective-permute-start.6
  58.0 14.8 %collective-permute-start.12 = (f32[18,1,128]{2,1,0:T(1,128)S(1)}, f32[18,1,128]{2,1,0:T(1,128)S(1)}, u32[]{:S(2)}, u32[]{:S(2)}) collective-permute-start(f32[18,1,128]{2,1,0:T(1,128)S(1)} %get-tuple-element.86), channel_id=1, source_target_pairs={{0,1},{1,2},{2,3},{3,4},{4,5},{5,6},{6,7},{7,8},{8,9},{9,10},{10,1... | collective-permute-start | bytes 27656 | tf_op jit(solution)/shard_map/ppermute | solution.py:24
  61.1 11.7 %collective-permute-start.13 = (f32[18,1,128]{2,1,0:T(1,128)S(1)}, f32[18,1,128]{2,1,0:T(1,128)S(1)}, u32[]{:S(2)}, u32[]{:S(2)}) collective-permute-start(f32[18,1,128]{2,1,0:T(1,128)S(1)} %get-tuple-element.87), channel_id=1, source_target_pairs={{1,0},{2,1},{3,2},{4,3},{5,4},{6,5},{7,6},{8,7},{9,8},{10,9},{11,1... | collective-permute-start | bytes 27656 | tf_op jit(solution)/shard_map/ppermute | solution.py:25
  81.0 7.0 collective-permute-start.16
  99.4 76.6 %collective-permute-start.18 = (f32[1,4,64]{2,0,1:T(1,128)S(1)}, f32[1,4,64]{2,0,1:T(1,128)S(1)}, u32[]{:S(2)}, u32[]{:S(2)}) collective-permute-start(f32[1,4,64]{2,0,1:T(1,128)S(1)} %get-tuple-element.139), channel_id=1, source_target_pairs={{0,32},{32,64},{64,96},{96,128},{128,160},{160,192},{192,224},{1,3... | collective-permute-start | bytes 3080 | tf_op jit(solution)/shard_map/ppermute | solution.py:24
  102.3 73.7 %collective-permute-start.19 = (f32[1,4,64]{2,0,1:T(1,128)S(1)}, f32[1,4,64]{2,0,1:T(1,128)S(1)}, u32[]{:S(2)}, u32[]{:S(2)}) collective-permute-start(f32[1,4,64]{2,0,1:T(1,128)S(1)} %get-tuple-element.140), channel_id=1, source_target_pairs={{32,0},{64,32},{96,64},{128,96},{160,128},{192,160},{224,192},{33,... | collective-permute-start | bytes 3080 | tf_op jit(solution)/shard_map/ppermute | solution.py:25
  214.9 72.6 %collective-permute-start.30 = (f32[1,4,64]{2,0,1:T(1,128)S(1)}, f32[1,4,64]{2,0,1:T(1,128)S(1)}, u32[]{:S(2)}, u32[]{:S(2)}) collective-permute-start(f32[1,4,64]{2,0,1:T(1,128)S(1)} %get-tuple-element.133), channel_id=1, source_target_pairs={{0,32},{32,64},{64,96},{96,128},{128,160},{160,192},{192,224},{1,3... | collective-permute-start | bytes 3080 | tf_op jit(solution)/shard_map/ppermute | solution.py:24
  218.9 68.6 %collective-permute-start.31 = (f32[1,4,64]{2,0,1:T(1,128)S(1)}, f32[1,4,64]{2,0,1:T(1,128)S(1)}, u32[]{:S(2)}, u32[]{:S(2)}) collective-permute-start(f32[1,4,64]{2,0,1:T(1,128)S(1)} %get-tuple-element.134), channel_id=1, source_target_pairs={{32,0},{64,32},{96,64},{128,96},{160,128},{192,160},{224,192},{33,... | collective-permute-start | bytes 3080 | tf_op jit(solution)/shard_map/ppermute | solution.py:25
  352.0 77.8 %collective-permute-start.48 = (f32[6,1,32]{2,0,1:T(8,128)S(1)}, f32[6,1,32]{2,0,1:T(8,128)S(1)}, u32[]{:S(2)}, u32[]{:S(2)}) collective-permute-start(f32[6,1,32]{2,0,1:T(8,128)S(1)} %get-tuple-element.149), channel_id=1, source_target_pairs={{0,1},{1,2},{2,3},{3,4},{4,5},{5,6},{6,7},{7,8},{8,9},{9,10},{10,1... | collective-permute-start | bytes 2312 | tf_op jit(solution)/shard_map/ppermute | solution.py:24
  355.4 74.4 %collective-permute-start.49 = (f32[6,1,32]{2,0,1:T(8,128)S(1)}, f32[6,1,32]{2,0,1:T(8,128)S(1)}, u32[]{:S(2)}, u32[]{:S(2)}) collective-permute-start(f32[6,1,32]{2,0,1:T(8,128)S(1)} %get-tuple-element.150), channel_id=1, source_target_pairs={{1,0},{2,1},{3,2},{4,3},{5,4},{6,5},{7,6},{8,7},{9,8},{10,9},{11,1... | collective-permute-start | bytes 2312 | tf_op jit(solution)/shard_map/ppermute | solution.py:25
  445.4 69.0 %collective-permute-start.54 = (f32[1,1,16]{2,0,1:T(1,128)S(1)}, f32[1,1,16]{2,0,1:T(1,128)S(1)}, u32[]{:S(2)}, u32[]{:S(2)}) collective-permute-start(f32[1,1,16]{2,0,1:T(1,128)S(1)} %get-tuple-element.204), channel_id=1, source_target_pairs={{0,32},{32,64},{64,96},{96,128},{128,160},{160,192},{192,224},{1,3... | collective-permute-start | bytes 200 | tf_op jit(solution)/shard_map/ppermute | solution.py:24
  448.3 66.1 %collective-permute-start.55 = (f32[1,1,16]{2,0,1:T(1,128)S(1)}, f32[1,1,16]{2,0,1:T(1,128)S(1)}, u32[]{:S(2)}, u32[]{:S(2)}) collective-permute-start(f32[1,1,16]{2,0,1:T(1,128)S(1)} %get-tuple-element.205), channel_id=1, source_target_pairs={{32,0},{64,32},{96,64},{128,96},{160,128},{192,160},{224,192},{33,... | collective-permute-start | bytes 200 | tf_op jit(solution)/shard_map/ppermute | solution.py:25
  711.4 7.3 collective-permute-start.88
  729.0 7.4 collective-permute-start.92
  746.7 7.4 collective-permute-start.96
  764.8 7.4 collective-permute-start.100
  782.6 7.4 collective-permute-start.104
  800.4 7.4 collective-permute-start.108
  818.1 7.3 collective-permute-start.112
  842.6 7.3 collective-permute-start.116
  860.4 7.3 collective-permute-start.120
  878.3 7.3 collective-permute-start.124
  896.1 7.3 collective-permute-start.128
  (111 other events, 550.6 us)
where the time goes:
time: 922 us; the launch traced here: 907 us
  starting transfers between devices  340 us (37%)
  blocking collectives  339 us (37%)
  waiting for transfers between devices  173 us (19%)
  local copies, waits for them, and re-layouts  34.2 us (4%)
  other arithmetic  17.6 us (2%)
    ppermute x64, starting transfers between devices, padded_2(): before = lax.ppermute(last, axis, up)  230 us
    ppermute x64, waiting for transfers between devices, padded_2(): after = lax.ppermute(initial, axis, down)  173 us
    ppermute x64, starting transfers between devices, padded_2(): after = lax.ppermute(initial, axis, down)  103 us
    all_gather x1, blocking collectives, shards(): lax.all_gather(own_z[None], ('gx', 'gy'), axis=0, tiled=True)  71.8 us
    all_gather x1, blocking collectives, shards(): lax.all_gather(own_alpha[None], ('gx', 'gy'), axis=0, tiled=True)  70.8 us
    all_gather x1, blocking collectives, shards(): lax.all_gather(own_x[:-1][None], ('gx', 'gy'), axis=0, tiled=True)  66.7 us
    all_gather x1, blocking collectives, shards(): gathered = lax.all_gather(resid[None], ('gx', 'gy'), axis=0, tiled=True)  66.3 us
    all_gather x1, blocking collectives, shards(): lax.all_gather(own_y[:, :-1][None], ('gx', 'gy'), axis=0, tiled=True)  63.8 us
  transfers between devices with their start and end apart: 130, of which 60 were waited for; matrix products, arithmetic and copies ran while one was open for 3% of the time, Pallas kernels for 0%

commit v1 on v0

v1 whole, which is shorter than its diff:
```python
import functools

import jax
import jax.numpy as jnp
from jax import lax
from jax.experimental import pallas as pl
from jax.experimental.pallas import tpu as pltpu
from jax.sharding import PartitionSpec as P

MESH = pl.DeviceIdType.MESH
F32 = jnp.float32

SHIFT = 0.002
LOW = 0.25
HIGH = 2.0
COARSE_LOW = 0.1
SWEEPS = 4
COARSE_SWEEPS = 12
GX = 8
GY = 32


def chebyshev_table(count, lower, upper):
    theta = (upper + lower) / 2.0
    delta = (upper - lower) / 2.0
    sigma = theta / delta
    rho_prev = 1.0 / sigma
    table = []
    for sweep in range(count):
        if sweep == 0:
            table.append((0.0, 1.0 / theta))
        else:
            rho_next = 1.0 / (2.0 * sigma - rho_prev)
            table.append((rho_next * rho_prev, 2.0 * rho_next / delta))
            rho_prev = rho_next
    return table


TABLE = chebyshev_table(SWEEPS, LOW, HIGH)
COARSE = chebyshev_table(COARSE_SWEEPS, COARSE_LOW, HIGH)

NEAR = [(-1, 0), (1, 0), (0, -1), (0, 1), (-1, -1), (-1, 1), (1, -1), (1, 1)]
FAR_Y = [(0, -2), (0, 2)]
FAR_XY = [(-1, -2), (-1, 2), (1, -2), (1, 2)]


def lanes(shape):
    return lax.broadcasted_iota(jnp.int32, shape, len(shape) - 1)


def roll(value, shift):
    shape = value.shape
    if len(shape) == 3:
        value = value.reshape(shape[0] * shape[1], shape[2])
    out = pltpu.roll(value, shift % 128, 1)
    return out.reshape(shape)


def partner(value, step):
    lane = lanes(value.shape)
    return jnp.where((lane // step) % 2 == 0, roll(value, -step), roll(value, step))


def pair_sum(value, step):
    return value + partner(value, step)


def pair_first(value, step):
    lane = lanes(value.shape)
    return jnp.where((lane // step) % 2 == 0, value, roll(value, step))


def choose(index, values):
    out = jnp.float32(values[-1])
    for i in range(len(values) - 2, -1, -1):
        out = jnp.where(index == i, jnp.float32(values[i]), out)
    return out


def kernel(
    f_in, al_in, bx_in, by_in, bz_in, out,
    b0, c0, v0, x0, t0, b1, c1, v1, x1, t1, pr,
    gc, g2, lin, a2, k2, v2, a3, k3, v3, a4, k4, v4,
    in_sem, ss, rs,
):
    gx = lax.axis_index("gx")
    gy = lax.axis_index("gy")
    counter = [0]

    def near(dx, dy):
        return (lax.rem(gx + dx + GX, GX), lax.rem(gy + dy + GY, GY))

    def gx_peer(i):
        return (lax.rem(gx + i, GX), gy)

    def gy_peer(i):
        return (gx, lax.rem(gy + i, GY))

    def remote(src, dst, index, device):
        return pltpu.make_async_remote_copy(
            src_ref=src, dst_ref=dst, send_sem=ss.at[index], recv_sem=rs.at[index],
            device_id=device, device_id_type=MESH,
        )

    def halo(view, sides, off_x, n_x, off_y, n_y, widths):
        copies = []
        for dx, dy in sides:
            first_x, last_x, first_y, last_y = widths(dx, dy)
            lo_x, w_x = (off_x, n_x) if dx == 0 else (off_x, first_x) if dx < 0 else (off_x + n_x - last_x, last_x)
            lo_y, w_y = (off_y, n_y) if dy == 0 else (off_y, first_y) if dy < 0 else (off_y + n_y - last_y, last_y)
            src = view(pl.ds(lo_x, w_x), pl.ds(lo_y, w_y))
            dst = view(pl.ds(lo_x - dx * n_x, w_x), pl.ds(lo_y - dy * n_y, w_y))
            copies.append(remote(src, dst, counter[0], near(dx, dy)))
            counter[0] += 1
        return copies

    def start(copies):
        for copy in copies:
            copy.start()

    def arrive(copies):
        for copy in copies:
            copy.wait_recv()

    def many(count, make):
        base = counter[0]
        counter[0] += count

        def each(what):
            def body(i, carry):
                what(make(i, base + i - 1))
                return carry

            lax.fori_loop(1, count + 1, body, 0)

        return each

    def own_rows(rows):
        return pl.ds(pl.multiple_of(8 * gy, 8), rows)

    def c2_gx(i, s):
        return remote(gc.at[gx, own_rows(8)], gc.at[gx, own_rows(8)], s, gx_peer(i))

    def c2_gy(i, s):
        return remote(gc.at[:, own_rows(8)], gc.at[:, own_rows(8)], s, gy_peer(i))

    def r2_gx(i, s):
        return remote(g2.at[gx, own_rows(2)], g2.at[gx, own_rows(2)], s, gx_peer(i))

    def r2_gy(i, s):
        return remote(g2.at[:, own_rows(2)], g2.at[:, own_rows(2)], s, gy_peer(i))

    send_b0 = halo(
        lambda x, y: b0.at[:, x, y], NEAR, 4, 16, 4, 8,
        lambda dx, dy: (5, 4, 5, 4) if dx == 0 or dy == 0 else (4, 4, 4, 4),
    )
    send_c1 = halo(
        lambda x, y: b1.at[pl.ds(1, 4), x, y], NEAR + FAR_Y + FAR_XY, 8, 8, 8, 4,
        lambda dx, dy: (2, 2, 2, 1) if abs(dy) == 2 else (6, 5, 4, 4),
    )
    send_f1 = halo(
        lambda x, y: b1.at[0, x, y], NEAR + FAR_Y + FAR_XY, 8, 8, 8, 4,
        lambda dx, dy: (1, 1, 1, 1) if abs(dy) == 2 else (5, 5, 4, 4),
    )
    send_x0 = halo(
        lambda x, y: x0.at[x, y], NEAR, 4, 16, 4, 8,
        lambda dx, dy: (4, 4, 4, 4) if dx == 0 or dy == 0 else (3, 3, 3, 3),
    )
    send_x1 = halo(
        lambda x, y: x1.at[x, y], NEAR + FAR_Y + FAR_XY, 8, 8, 8, 4,
        lambda dx, dy: (2, 2, 2, 2) if abs(dy) == 2 else (6, 6, 4, 4),
    )
    send_c2a = many(GX - 1, c2_gx)
    send_c2b = many(GY - 1, c2_gy)
    send_r2a = many(GX - 1, r2_gx)
    send_r2b = many(GY - 1, r2_gy)

    inputs = [
        pltpu.make_async_copy(ref, b0.at[i, pl.ds(4, 16), pl.ds(4, 8)], in_sem.at[i])
        for i, ref in enumerate((f_in, al_in, bx_in, by_in, bz_in))
    ]
    start(inputs)
    barrier = pltpu.get_barrier_semaphore()

    def greet(device):
        pl.semaphore_signal(barrier, inc=1, device_id=device, device_id_type=MESH)

    def greet_gx(i, carry):
        greet(gx_peer(i))
        return carry

    def greet_gy(i, carry):
        greet(gy_peer(i))
        return carry

    diagonal = [side for side in NEAR + FAR_XY if side[0] and side[1]]
    lax.fori_loop(1, GX, greet_gx, 0)
    lax.fori_loop(1, GY, greet_gy, 0)
    for dx, dy in diagonal:
        greet(near(dx, dy))

    for ref in (a2, a3, a4, v2, v3, v4, lin):
        flat = ref
        edge = jnp.zeros((32, 128), F32)
        if len(ref.shape) == 3:
            flat[0] = jnp.zeros(ref.shape[1:], F32)
            flat[GX + 1] = jnp.zeros(ref.shape[1:], F32)

            def rows_of(i, carry, flat=flat):
                flat[i, 0:8] = jnp.zeros((8, 128), F32)
                flat[i, 72:80] = jnp.zeros((8, 128), F32)
                return carry

            lax.fori_loop(1, GX + 1, rows_of, 0)
        else:

            def clear(i, carry, flat=flat, edge=edge):
                p, q = i // flat.shape[1], i % flat.shape[1]
                flat[p, q, 0] = edge
                flat[p, q, GX + 1] = edge
                flat[p, q, 1 : GX + 1, 0:8] = jnp.zeros((GX, 8, 128), F32)
                flat[p, q, 1 : GX + 1, 24:32] = jnp.zeros((GX, 8, 128), F32)
                return carry

            lax.fori_loop(0, flat.shape[0] * flat.shape[1], clear, 0)
    for copy in inputs:
        copy.wait()

    def split_slots(value):
        pairs = value.reshape(value.shape[0] // 2, 2, *value.shape[1:])
        return pairs[:, 0], pairs[:, 1]

    def coarsen(ref, lo, n, off, rows, step, first):
        def take(i, odd):
            return split_slots(ref[i, pl.ds(lo, n), pl.ds(off + odd, rows // 2, stride=2)])

        result = []
        for name in range(4):
            i = first + name
            even_a, even_b = take(i, 0)
            if name == 2:
                value = pair_sum(even_a + even_b, step) * 0.25
            else:
                odd_a, odd_b = take(i, 1)
                if name == 0:
                    value = pair_sum((even_a + even_b) + (odd_a + odd_b), step) * 0.125
                elif name == 1:
                    value = pair_sum(even_a + odd_a, step) * 0.25
                else:
                    value = pair_first((even_a + even_b) + (odd_a + odd_b), step) * 0.25
            result.append(value)
        return result

    for i, value in enumerate(coarsen(b0, 4, 16, 4, 8, 1, 1)):
        b1[1 + i, 8:16, 8:12] = value

    def pack(value):
        lane = lanes(value.shape[1:]) % 4
        packed = value[3]
        for i in range(2, -1, -1):
            packed = jnp.where(lane == i, value[i], packed)
        return packed

    packed = [pack(value) for value in coarsen(b1, 8, 8, 8, 4, 2, 1)]
    for i in range(4):
        gc[gx, pl.ds(8 * gy + 2 * i, 2)] = packed[i]

    pl.semaphore_wait(barrier, GX - 1 + GY - 1 + len(diagonal))

    start(send_b0)
    send_c2a(lambda copy: copy.start())
    start(send_c1)
    send_c2a(lambda copy: copy.wait_recv())
    send_c2b(lambda copy: copy.start())

    def valid(s, rows, off_x, n_x, off_y, n_y):
        x = gx * n_x + s - off_x
        y = gy * n_y + lax.broadcasted_iota(jnp.int32, (16, 128), 0) + rows - off_y
        inside = jnp.logical_and(y >= 0, y < GY * n_y)
        return jnp.logical_and(inside, jnp.logical_and(x >= 0, x < GX * n_x)), x, y

    def slots(lo, hi, body, unroll=2):
        def run(s, carry):
            body(s)
            return carry

        lax.fori_loop(lo, hi, run, 0, unroll=unroll)

    def prepare(b, c, row, scale, step, n_x, n_y, off, lo, hi):
        lane = lanes((16, 128))

        def body(s):
            ok, x, y = valid(s, row, off, n_x, off, n_y)
            low_x, low_y, low_z = b[2, s, pl.ds(row, 16)], b[3, s, pl.ds(row, 16)], b[4, s, pl.ds(row, 16)]
            up_x = jnp.where(x + 1 < GX * n_x, b[2, s + 1, pl.ds(row, 16)], 0.0)
            up_y = jnp.where(y + 1 < GY * n_y, b[3, s, pl.ds(row + 1, 16)], 0.0)
            up_z = jnp.where(lane >= 128 - step, 0.0, roll(low_z, -step))
            diagonal = SHIFT * b[1, s, pl.ds(row, 16)] + scale * (low_x + up_x + low_y + up_y + low_z + up_z)
            inverse = jnp.where(ok, 1.0 / diagonal, 0.0)
            scaled = scale * inverse
            c[1, s] = low_x * scaled
            c[2, s] = up_x * scaled
            c[3, s] = low_y * scaled
            c[4, s] = up_y * scaled
            c[5, s] = jnp.where(lane < step, 0.0, low_z * scaled)
            c[6, s] = up_z * scaled
            c[7, s] = diagonal
            c[8, s] = inverse

        slots(lo, hi, body)

    def scaled_residual(c, v, a, s, step, rows=16, off=0):
        at = pl.ds(8 + off, rows)
        centre = v[a, s + 1, at]
        k = pl.ds(off, rows)
        total = c[0, s, k] - centre
        along_x = c[1, s, k] * v[a, s, at] + c[2, s, k] * v[a, s + 2, at]
        along_y = c[3, s, k] * v[a, s + 1, pl.ds(7 + off, rows)] + c[4, s, k] * v[a, s + 1, pl.ds(9 + off, rows)]
        along_z = c[5, s, k] * roll(centre, step) + c[6, s, k] * roll(centre, -step)
        return centre, total + (along_x + along_y) + along_z

    def sweep(c, v, a, s, step, k, first):
        keep, gain = TABLE[k]
        centre, r = scaled_residual(c, v, a, s, step)
        change = gain * r
        if not first:
            change = change + keep * (centre - v[1 - a, s + 1, pl.ds(8, 16)])
        return centre + change

    def smooth_up(b, c, v, row, step, lo, hi, more=0):
        def begin(s):
            g = b[0, s, pl.ds(row, 16)] * c[8, s]
            c[0, s] = g
            v[0, s + 1, pl.ds(8, 16)] = TABLE[0][1] * g

        slots(lo - more, hi + more, begin)

        def second(s):
            keep, gain = TABLE[1]
            centre, r = scaled_residual(c, v, 0, s, step)
            v[1, s + 1, pl.ds(8, 16)] = centre + gain * r + keep * centre

        slots(lo + 1, hi - 1, second)
        for k in (2, 3):
            a = (k - 1) % 2

            def body(s, k=k, a=a):
                v[1 - a, s + 1, pl.ds(8, 16)] = sweep(c, v, a, s, step, k, False)

            slots(lo + k, hi - k, body)

    arrive(send_b0)
    prepare(b0, c0, 0, 1.0, 1, 16, 8, 4, 0, 24)
    smooth_up(b0, c0, v0, 0, 1, 0, 24)

    def resid0(i):
        total = None
        for j in range(2):
            s = 4 + 2 * i + j
            centre, r = scaled_residual(c0, v0, 1, s, 1, 8, 4)
            x0[s, 4:12] = centre
            r = r * c0[7, s, 4:12]
            total = r if total is None else total + r
        t0[i] = total

    slots(0, 8, resid0)
    both = t0[:, pl.ds(0, 4, stride=2)] + t0[:, pl.ds(1, 4, stride=2)]
    b1[0, 8:16, 8:12] = pair_sum(both, 1) * 0.125
    start(send_f1)
    start(send_x0)

    arrive(send_c1)
    prepare(b1, c1, 2, 0.25, 2, 8, 4, 8, 2, 22)
    arrive(send_f1)

    smooth_up(b1, c1, v1, 2, 2, 4, 20, 1)

    def resid1(i):
        total = None
        for j in range(2):
            s = 8 + 2 * i + j
            centre, r = scaled_residual(c1, v1, 1, s, 2, 4, 6)
            x1[s, 8:12] = centre
            r = r * c1[7, s, 6:10]
            total = r if total is None else total + r
        t1[i, 0:4] = total

    slots(0, 4, resid1)
    both = t1[:, pl.ds(0, 2, stride=2)] + t1[:, pl.ds(1, 2, stride=2)]
    g2[gx, own_rows(2)] = pack(pair_sum(both, 2) * 0.125)
    send_r2a(lambda copy: copy.start())
    start(send_x1)

    shape = (GX, 16, 128)
    lane = lanes(shape)
    lane4 = lane % 4

    def get(ref, lead, q, dx=0, dy=0):
        planes = ref.shape[1]
        row = 8
        if q + dy >= planes:
            q, row = 0, 9
        elif q + dy < 0:
            q, row = planes - 1, 7
        else:
            q = q + dy
        return ref[lead, q, pl.ds(1 + dx, GX), pl.ds(row, 16)]

    def x_next(ref, lead, q, level):
        if level == 4:
            return get(ref, lead, q, 1)
        centre, beyond = get(ref, lead, q), get(ref, lead, q, 1)
        if level == 2:
            return jnp.where(lane4 < 3, roll(centre, -1), roll(beyond, 3))
        return jnp.where(lane4 < 2, roll(centre, -2), roll(beyond, 2))

    def x_last(ref, lead, q, level):
        if level == 4:
            return get(ref, lead, q, -1)
        centre, beyond = get(ref, lead, q), get(ref, lead, q, -1)
        if level == 2:
            return jnp.where(lane4 > 0, roll(centre, 1), roll(beyond, -3))
        return jnp.where(lane4 >= 2, roll(centre, 2), roll(beyond, -2))

    def prepare_whole(a, c, level):
        scale = 0.25**level
        step = 2**level
        for q in range(a.shape[1]):
            low_x, low_y, low_z = get(a, 1, q), get(a, 2, q), get(a, 3, q)
            up_x = x_next(a, 1, q, level)
            up_y = get(a, 2, q, 0, 1)
            up_z = jnp.where(lane >= 128 - step, 0.0, roll(low_z, -step))
            diagonal = SHIFT * get(a, 0, q) + scale * (low_x + up_x + low_y + up_y + low_z + up_z)
            inverse = 1.0 / diagonal
            scaled = scale * inverse
            c[1, q] = low_x * scaled
            c[2, q] = up_x * scaled
            c[3, q] = low_y * scaled
            c[4, q] = up_y * scaled
            c[5, q] = jnp.where(lane < step, 0.0, low_z * scaled)
            c[6, q] = up_z * scaled
            c[7, q] = diagonal
            c[8, q] = inverse

    def inner(ref, lead, q, value):
        ref[lead, q, pl.ds(1, GX), pl.ds(8, 16)] = value

    def coarsen_whole(fine, coarse, z_step, x_step):
        for p in range(coarse.shape[1]):
            for name in range(4):
                value = get(fine, name, 2 * p)
                if name != 2:
                    value = value + get(fine, name, 2 * p + 1)
                value = pair_first(value, z_step) if name == 3 else pair_sum(value, z_step)
                value = pair_first(value, x_step) if name == 1 else pair_sum(value, x_step)
                inner(coarse, name, p, value * (0.125 if name == 0 else 0.25))

    def whole_residual(c, v, a, q, level):
        step = 2**level
        centre = get(v, a, q)
        total = c[0, q] - centre
        along_x = c[1, q] * x_last(v, a, q, level) + c[2, q] * x_next(v, a, q, level)
        along_y = c[3, q] * get(v, a, q, 0, -1) + c[4, q] * get(v, a, q, 0, 1)
        along_z = c[5, q] * roll(centre, step) + c[6, q] * roll(centre, -step)
        return centre, total + (along_x + along_y) + along_z

    def sweeps_whole(c, v, level, table, lo, hi):
        def body(k, carry):
            keep = choose(k, [entry[0] for entry in table])
            gain = choose(k, [entry[1] for entry in table])
            new = lax.rem(k, 2)
            old = 1 - new
            for q in range(v.shape[1]):
                centre, r = whole_residual(c, v, old, q, level)
                inner(v, new, q, centre + (gain * r + keep * (centre - get(v, new, q))))
            return carry

        lax.fori_loop(lo, hi, body, 0)

    def begin_whole(c, v, table, q, f):
        g = f * c[8, q]
        c[0, q] = g
        inner(v, 0, q, table[0][1] * g)
        inner(v, 1, q, jnp.zeros(shape, F32))

    def down(c, v, coarse_c, coarse_v, level, coarse_table):
        sweeps_whole(c, v, level, TABLE, 1, SWEEPS)
        for p in range(coarse_v.shape[1]):
            total = None
            for q in (2 * p, 2 * p + 1):
                _, r = whole_residual(c, v, 1, q, level)
                r = r * c[7, q]
                total = r if total is None else total + r
            total = pair_sum(pair_sum(total, 2**level), level - 1) * 0.125
            begin_whole(coarse_c, coarse_v, coarse_table, p, total)

    def up(c, v, coarse_v, level):
        for q in range(v.shape[1]):
            inner(v, 1, q, get(v, 1, q) + get(coarse_v, 1, q // 2))
        sweeps_whole(c, v, level, TABLE, 0, SWEEPS)

    send_c2b(lambda copy: copy.wait_recv())
    for q in range(4):
        for name in range(4):
            inner(a2, name, q, gc[:, pl.ds(8 * (q // 2) + 2 * name + q % 2, 16, stride=16)])
    prepare_whole(a2, k2, 2)
    send_r2a(lambda copy: copy.wait_recv())
    send_r2b(lambda copy: copy.start())
    coarsen_whole(a2, a3, 4, 1)
    prepare_whole(a3, k3, 3)
    coarsen_whole(a3, a4, 8, 2)
    prepare_whole(a4, k4, 4)
    send_r2b(lambda copy: copy.wait_recv())

    for q in range(4):
        begin_whole(k2, v2, TABLE, q, g2[:, pl.ds(8 * (q // 2) + q % 2, 16, stride=16)])
    down(k2, v2, k3, v3, 2, TABLE)
    down(k3, v3, k4, v4, 3, COARSE)
    sweeps_whole(k4, v4, 4, COARSE, 1, COARSE_SWEEPS)
    up(k3, v3, v4, 3)
    up(k2, v2, v3, 2)

    for q in range(4):
        lin[pl.ds(1, GX), pl.ds(8 + q, 16, stride=4)] = get(v2, 1, q)
    arrive(send_x1)
    lane_row = lanes((8, 128)) % 4

    def spread(block):
        value = lin[gx + block, pl.ds(8 + 2 * gy - 3, 8)]
        for x in range(4):
            one = jnp.where(lane_row == x, value, 0.0)
            one = pair_sum(pair_sum(one, 1), 2)
            pr[4 * block + x, pl.ds(0, 8, stride=2)] = one
            pr[4 * block + x, pl.ds(1, 8, stride=2)] = one

    slots(0, 3, spread, 1)

    def correct1(s):
        ok, _, _ = valid(s, 2, 8, 8, 8, 4)
        v1[0, s + 1, pl.ds(8, 16)] = jnp.where(ok, x1[s, pl.ds(2, 16)] + pr[s // 2], 0.0)

    slots(2, 22, correct1)

    def smooth_down(c, v, step, lo, hi, last):
        for k in range(SWEEPS):
            a = k % 2

            def body(s, k=k, a=a):
                value = sweep(c, v, a, s, step, k, k == 0)
                if k == SWEEPS - 1:
                    last(s, value)
                else:
                    v[1 - a, s + 1, pl.ds(8, 16)] = value

            slots(lo + k, hi - k, body)

    def spread0(s, value):
        t1[s - 6] = value[4:12]

    smooth_down(c1, v1, 2, 3, 21, spread0)

    def widen(i):
        pr[i, pl.ds(0, 8, stride=2)] = t1[i]
        pr[i, pl.ds(1, 8, stride=2)] = t1[i]

    slots(0, 12, widen)
    arrive(send_x0)

    def correct0(s):
        ok, _, _ = valid(s, 0, 4, 16, 4, 8)
        v0[0, s + 1, pl.ds(8, 16)] = jnp.where(ok, x0[s] + pr[s // 2], 0.0)

    slots(0, 24, correct0)

    def finish(s, value):
        out[s - 4] = value[4:12]

    smooth_down(c0, v0, 1, 1, 23, finish)

    for copy in send_b0 + send_c1 + send_f1 + send_x0 + send_x1:
        copy.wait_send()
    for each in (send_c2a, send_c2b, send_r2a, send_r2b):
        each(lambda copy: copy.wait_send())


def step(right_side, alpha, beta_x, beta_y, beta_z):
    copies = 8 + 14 + 14 + 8 + 14 + 2 * (GX - 1 + GY - 1)
    vmem = [
        (5, 25, 24, 128),
        (9, 24, 16, 128),
        (2, 26, 32, 128),
        (24, 16, 128),
        (8, 8, 128),
        (5, 25, 24, 128),
        (9, 24, 16, 128),
        (2, 26, 32, 128),
        (24, 24, 128),
        (12, 8, 128),
        (12, 16, 128),
        (GX, 8 * GY, 128),
        (GX, 8 * GY, 128),
        (GX + 2, 80, 128),
    ]
    for planes in (4, 2, 1):
        vmem += [(4, planes, GX + 2, 32, 128), (9, planes, GX, 16, 128), (2, planes, GX + 2, 32, 128)]
    return pl.pallas_call(
        kernel,
        out_shape=jax.ShapeDtypeStruct((16, 8, 128), F32),
        in_specs=[pl.BlockSpec(memory_space=pl.ANY)] * 5,
        out_specs=pl.BlockSpec(memory_space=pltpu.VMEM),
        scratch_shapes=[pltpu.VMEM(shape, F32) for shape in vmem]
        + [
            pltpu.SemaphoreType.DMA((5,)),
            pltpu.SemaphoreType.DMA((copies,)),
            pltpu.SemaphoreType.DMA((copies,)),
        ],
        compiler_params=pltpu.CompilerParams(
            collective_id=0, has_side_effects=True, vmem_limit_bytes=48 * 1024 * 1024
        ),
        name="vcycle",
    )(right_side, alpha, beta_x, beta_y, beta_z)


def solution(mesh):
    spec = P("gx", "gy", None)
    return jax.shard_map(step, mesh=mesh, in_specs=(spec,) * 5, out_specs=spec, check_vma=False)
```

time: 922 us -> 71.9 us (0.08); the launches traced: 907 us -> 71.6 us
  starting transfers between devices: 340 us -> 0 us
  blocking collectives: 339 us -> 0 us
  waiting for transfers between devices: 173 us -> 0 us
  Pallas kernels: 0 us -> 66.8 us
  local copies, waits for them, and re-layouts: 34.2 us -> 4.83 us
  other arithmetic: 17.6 us -> 0 us
    ppermute x130 -> x0, starting transfers between devices: 340 us -> none  [the longest x64 230 us: padded_2(): before = lax.ppermute(last, axis, up)]
    all_gather x5 -> x0, blocking collectives: 339 us -> none  [the longest x1 71.8 us: shards(): lax.all_gather(own_z[None], ('gx', 'gy'), axis=0, tiled=True)]
    ppermute x130 -> x0, waiting for transfers between devices: 173 us -> none  [the longest x64 173 us: padded_2(): after = lax.ppermute(initial, axis, down)]
    pallas_call x0 -> x1, Pallas kernels: none -> 66.8 us  [step(): pl.pallas_call(kernel, out_shape=jax.ShapeDtypeStruct((16, 8, 128), F32),...]
    reshape x10 -> x0, local copies, waits for them, and re-layouts: 18.5 us -> none  [the longest x3 12.5 us: restrict_cells(): values.reshape(size_x // 2, 2, size_y // 2, 2, size_z // 2, 2)]
  transfers between devices with their start and end apart: 130 -> 0, of which waited for: 60 -> 0; matrix products, arithmetic and copies ran while one was open for 3% -> 0% of each run, Pallas kernels for 0% -> 0%
where the time goes in v1:
time: 71.9 us; the launch traced here: 71.6 us
  Pallas kernels  66.8 us (93%)
  local copies, waits for them, and re-layouts  4.83 us (7%)
    pallas_call x1, Pallas kernels, step(): pl.pallas_call(kernel, out_shape=jax.ShapeDtypeStruct((16, 8, 128), F32),...  66.8 us
    unnamed x11, local copies, waits for them, and re-layouts  4.83 us

profile of v1, /device:TPU:1, one launch (start us, length us, event | category | flops | bytes accessed | tf_op | source)
XLA Modules:
  0.0 71.6 jit_solution(11221462517738156391)
XLA Ops:
  0.0 0.0 copy-start
  0.0 0.8 %copy-done = f32[16,8,128]{2,1,0:T(8,128)S(1)} copy-done((f32[16,8,128]{2,1,0:T(8,128)S(1)}, f32[16,8,128]{2,1,0:T(8,128)}, u32[]{:S(2)}) %copy-start) | copy-done | bytes 65560
  0.8 0.0 copy-start.1
  0.8 0.8 %copy-done.1 = f32[16,8,128]{2,1,0:T(8,128)S(1)} copy-done((f32[16,8,128]{2,1,0:T(8,128)S(1)}, f32[16,8,128]{2,1,0:T(8,128)}, u32[]{:S(2)}) %copy-start.1) | copy-done | bytes 65560
  1.7 0.0 copy-start.2
  1.7 0.8 %copy-done.2 = f32[16,8,128]{2,1,0:T(8,128)S(1)} copy-done((f32[16,8,128]{2,1,0:T(8,128)S(1)}, f32[16,8,128]{2,1,0:T(8,128)}, u32[]{:S(2)}) %copy-start.2) | copy-done | bytes 65560
  2.5 0.0 copy-start.3
  2.5 0.8 %copy-done.3 = f32[16,8,128]{2,1,0:T(8,128)S(1)} copy-done((f32[16,8,128]{2,1,0:T(8,128)S(1)}, f32[16,8,128]{2,1,0:T(8,128)}, u32[]{:S(2)}) %copy-start.3) | copy-done | bytes 65560
  3.4 0.0 copy-start.4
  3.4 0.8 %copy-done.4 = f32[16,8,128]{2,1,0:T(8,128)S(1)} copy-done((f32[16,8,128]{2,1,0:T(8,128)S(1)}, f32[16,8,128]{2,1,0:T(8,128)}, u32[]{:S(2)}) %copy-start.4) | copy-done | bytes 65560
  4.2 66.8 %vcycle.1 = f32[16,8,128]{2,1,0:T(8,128)S(1)} custom-call(f32[16,8,128]{2,1,0:T(8,128)S(1)} %copy-done, f32[16,8,128]{2,1,0:T(8,128)S(1)} %copy-done.1, f32[16,8,128]{2,1,0:T(8,128)S(1)} %copy-done.2, f32[16,8,128]{2,1,0:T(8,128)S(1)} %copy-done.3, f32[16,8,128]{2,1,0:T(8,128)S(1)} %copy-done.4), custom_call_target="tpu_custom_call" | custom-call | tf_op jit(solution)/shard_map/vcycle/pallas_call | solution.py:606
  71.0 0.6 copy.7
Async XLA Ops:
  0.0 0.8 %copy-start = (f32[16,8,128]{2,1,0:T(8,128)S(1)}, f32[16,8,128]{2,1,0:T(8,128)}, u32[]{:S(2)}) copy-start(f32[16,8,128]{2,1,0:T(8,128)} %f_in.1) | copy-start | bytes 196612
  0.8 0.8 %copy-start.1 = (f32[16,8,128]{2,1,0:T(8,128)S(1)}, f32[16,8,128]{2,1,0:T(8,128)}, u32[]{:S(2)}) copy-start(f32[16,8,128]{2,1,0:T(8,128)} %al_in.1) | copy-start | bytes 196612
  1.7 0.8 %copy-start.2 = (f32[16,8,128]{2,1,0:T(8,128)S(1)}, f32[16,8,128]{2,1,0:T(8,128)}, u32[]{:S(2)}) copy-start(f32[16,8,128]{2,1,0:T(8,128)} %bx_in.1) | copy-start | bytes 196612
  2.5 0.8 %copy-start.3 = (f32[16,8,128]{2,1,0:T(8,128)S(1)}, f32[16,8,128]{2,1,0:T(8,128)}, u32[]{:S(2)}) copy-start(f32[16,8,128]{2,1,0:T(8,128)} %by_in.1) | copy-start | bytes 196612
  3.4 0.8 %copy-start.4 = (f32[16,8,128]{2,1,0:T(8,128)S(1)}, f32[16,8,128]{2,1,0:T(8,128)}, u32[]{:S(2)}) copy-start(f32[16,8,128]{2,1,0:T(8,128)} %bz_in.1) | copy-start | bytes 196612

commit v2 on v1

--- a/solution.py
+++ b/solution.py
@@ -142,13 +142,14 @@
         return remote(gc.at[gx, own_rows(8)], gc.at[gx, own_rows(8)], s, gx_peer(i))
 
     def c2_gy(i, s):
-        return remote(gc.at[:, own_rows(8)], gc.at[:, own_rows(8)], s, gy_peer(i))
+        return remote(gc.at[:, own_rows(8)], gc.at[:, own_rows(8)], s, gy_peer(2 * i))
+
+    def c2_core(i, s):
+        rows = pl.ds(pl.multiple_of(8 * lax.rem(gy - 2 * (i - 1) + GY, GY), 8), 8)
+        return remote(gc.at[:, rows], gc.at[:, rows], s, (gx, gy + 1 - 2 * lax.rem(gy, 2)))
 
     def r2_gx(i, s):
         return remote(g2.at[gx, own_rows(2)], g2.at[gx, own_rows(2)], s, gx_peer(i))
-
-    def r2_gy(i, s):
-        return remote(g2.at[:, own_rows(2)], g2.at[:, own_rows(2)], s, gy_peer(i))
 
     send_b0 = halo(
         lambda x, y: b0.at[:, x, y], NEAR, 4, 16, 4, 8,
@@ -159,21 +160,31 @@
         lambda dx, dy: (2, 2, 2, 1) if abs(dy) == 2 else (6, 5, 4, 4),
     )
     send_f1 = halo(
-        lambda x, y: b1.at[0, x, y], NEAR + FAR_Y + FAR_XY, 8, 8, 8, 4,
-        lambda dx, dy: (1, 1, 1, 1) if abs(dy) == 2 else (5, 5, 4, 4),
+        lambda x, y: b1.at[0, x, y], NEAR, 8, 8, 8, 4,
+        lambda dx, dy: (4, 4, 4, 4) if dx == 0 or dy == 0 else (3, 3, 3, 3),
     )
     send_x0 = halo(
         lambda x, y: x0.at[x, y], NEAR, 4, 16, 4, 8,
         lambda dx, dy: (4, 4, 4, 4) if dx == 0 or dy == 0 else (3, 3, 3, 3),
     )
     send_x1 = halo(
-        lambda x, y: x1.at[x, y], NEAR + FAR_Y + FAR_XY, 8, 8, 8, 4,
+        lambda x, y: x1.at[:, x, y], NEAR + FAR_Y + FAR_XY, 8, 8, 8, 4,
         lambda dx, dy: (2, 2, 2, 2) if abs(dy) == 2 else (6, 6, 4, 4),
     )
     send_c2a = many(GX - 1, c2_gx)
-    send_c2b = many(GY - 1, c2_gy)
+    c2b_base = counter[0]
+    send_c2b = many(GY // 2 - 1, c2_gy)
+    send_c2c = many(GY // 2, c2_core)
     send_r2a = many(GX - 1, r2_gx)
-    send_r2b = many(GY - 1, r2_gy)
+    send_r2b = []
+    for a, b, e in sorted(
+        [(a, b, e) for a in range(4) for b in range(4) for e in range(2) if a + b + e],
+        key=lambda t: -(2 * min(t[0], 4 - t[0]) + 2 * min(t[1], 4 - t[1]) + t[2]),
+    ):
+        x, y, core = lax.rem(gy // 8 + a, 4), lax.rem(gy // 2 + b, 4), lax.rem(gy + e, 2)
+        own = g2.at[:, own_rows(2)]
+        send_r2b.append(remote(own, own, counter[0], (gx, 8 * x + 2 * y + core)))
+        counter[0] += 1
 
     inputs = [
         pltpu.make_async_copy(ref, b0.at[i, pl.ds(4, 16), pl.ds(4, 8)], in_sem.at[i])
@@ -199,30 +210,19 @@
     for dx, dy in diagonal:
         greet(near(dx, dy))
 
-    for ref in (a2, a3, a4, v2, v3, v4, lin):
-        flat = ref
-        edge = jnp.zeros((32, 128), F32)
-        if len(ref.shape) == 3:
-            flat[0] = jnp.zeros(ref.shape[1:], F32)
-            flat[GX + 1] = jnp.zeros(ref.shape[1:], F32)
-
-            def rows_of(i, carry, flat=flat):
-                flat[i, 0:8] = jnp.zeros((8, 128), F32)
-                flat[i, 72:80] = jnp.zeros((8, 128), F32)
-                return carry
-
-            lax.fori_loop(1, GX + 1, rows_of, 0)
-        else:
-
-            def clear(i, carry, flat=flat, edge=edge):
-                p, q = i // flat.shape[1], i % flat.shape[1]
-                flat[p, q, 0] = edge
-                flat[p, q, GX + 1] = edge
-                flat[p, q, 1 : GX + 1, 0:8] = jnp.zeros((GX, 8, 128), F32)
-                flat[p, q, 1 : GX + 1, 24:32] = jnp.zeros((GX, 8, 128), F32)
-                return carry
-
-            lax.fori_loop(0, flat.shape[0] * flat.shape[1], clear, 0)
+    edge = jnp.zeros((32, 128), F32)
+    side = jnp.zeros((GX, 8, 128), F32)
+    for ref in (a2, a3, a4, v2, v3, v4):
+
+        def clear(i, carry, ref=ref):
+            p, q = i // ref.shape[1], i % ref.shape[1]
+            ref[p, q, 0] = edge
+            ref[p, q, GX + 1] = edge
+            ref[p, q, 1 : GX + 1, 0:8] = side
+            ref[p, q, 1 : GX + 1, 24:32] = side
+            return carry
+
+        lax.fori_loop(0, ref.shape[0] * ref.shape[1], clear, 0)
     for copy in inputs:
         copy.wait()
 
@@ -279,7 +279,7 @@
         inside = jnp.logical_and(y >= 0, y < GY * n_y)
         return jnp.logical_and(inside, jnp.logical_and(x >= 0, x < GX * n_x)), x, y
 
-    def slots(lo, hi, body, unroll=2):
+    def slots(lo, hi, body, unroll=4):
         def run(s, carry):
             body(s)
             return carry
@@ -327,13 +327,13 @@
             change = change + keep * (centre - v[1 - a, s + 1, pl.ds(8, 16)])
         return centre + change
 
-    def smooth_up(b, c, v, row, step, lo, hi, more=0):
+    def smooth_up(b, c, v, row, step, lo, hi):
         def begin(s):
             g = b[0, s, pl.ds(row, 16)] * c[8, s]
             c[0, s] = g
             v[0, s + 1, pl.ds(8, 16)] = TABLE[0][1] * g
 
-        slots(lo - more, hi + more, begin)
+        slots(lo, hi, begin)
 
         def second(s):
             keep, gain = TABLE[1]
@@ -365,22 +365,34 @@
 
     slots(0, 8, resid0)
     both = t0[:, pl.ds(0, 4, stride=2)] + t0[:, pl.ds(1, 4, stride=2)]
-    b1[0, 8:16, 8:12] = pair_sum(both, 1) * 0.125
+    f1 = pair_sum(both, 1) * 0.125
+    b1[0, 8:16, 8:12] = f1
+    x1[1, 8:16, 8:12] = f1
     start(send_f1)
     start(send_x0)
 
     arrive(send_c1)
     prepare(b1, c1, 2, 0.25, 2, 8, 4, 8, 2, 22)
+
+    def forward(i, carry):
+        @pl.when(i > 1)
+        def _():
+            c2_gy(i - 1, c2b_base + i - 2).wait_recv()
+
+        c2_core(i, c2b_base + GY // 2 + i - 2).start()
+        return carry
+
+    lax.fori_loop(1, GY // 2 + 1, forward, 0)
     arrive(send_f1)
 
-    smooth_up(b1, c1, v1, 2, 2, 4, 20, 1)
+    smooth_up(b1, c1, v1, 2, 2, 4, 20)
 
     def resid1(i):
         total = None
         for j in range(2):
             s = 8 + 2 * i + j
             centre, r = scaled_residual(c1, v1, 1, s, 2, 4, 6)
-            x1[s, 8:12] = centre
+            x1[0, s, 8:12] = centre
             r = r * c1[7, s, 6:10]
             total = r if total is None else total + r
         t1[i, 0:4] = total
@@ -391,11 +403,12 @@
     send_r2a(lambda copy: copy.start())
     start(send_x1)
 
-    shape = (GX, 16, 128)
-    lane = lanes(shape)
-    lane4 = lane % 4
-
-    def get(ref, lead, q, dx=0, dy=0):
+    HALVES = [(0, GX, 0, 8), (0, GX, 8, 8)]
+
+    def lane_of(value):
+        return lanes(value.shape)
+
+    def get(ref, lead, q, win, dy=0, wide=False):
         planes = ref.shape[1]
         row = 8
         if q + dy >= planes:
@@ -404,129 +417,158 @@
             q, row = planes - 1, 7
         else:
             q = q + dy
-        return ref[lead, q, pl.ds(1 + dx, GX), pl.ds(row, 16)]
-
-    def x_next(ref, lead, q, level):
+        x0, nx, r0, nr = win
+        start, count = (x0, nx + 2) if wide else (x0 + 1, nx)
+        return ref[lead, q, pl.ds(start, count), pl.ds(row + r0, nr)]
+
+    def put(ref, lead, q, win, value):
+        x0, nx, r0, nr = win
+        ref[lead, q, pl.ds(x0 + 1, nx), pl.ds(8 + r0, nr)] = value
+
+    def x_next(wide, level):
         if level == 4:
-            return get(ref, lead, q, 1)
-        centre, beyond = get(ref, lead, q), get(ref, lead, q, 1)
+            return wide[2:]
+        lane4 = lane_of(wide[1:-1]) % 4
         if level == 2:
-            return jnp.where(lane4 < 3, roll(centre, -1), roll(beyond, 3))
-        return jnp.where(lane4 < 2, roll(centre, -2), roll(beyond, 2))
-
-    def x_last(ref, lead, q, level):
+            return roll(jnp.where(lane4 == 0, roll(wide[2:], 4), wide[1:-1]), -1)
+        return jnp.where(lane4 < 2, roll(wide[1:-1], -2), roll(wide[2:], 2))
+
+    def around(wide, level):
+        step = 2**level
+        centre = wide[1:-1]
+        lane4 = lane_of(centre) % 4
         if level == 4:
-            return get(ref, lead, q, -1)
-        centre, beyond = get(ref, lead, q), get(ref, lead, q, -1)
+            return wide[:-2], wide[2:], roll(centre, step), roll(centre, -step)
         if level == 2:
-            return jnp.where(lane4 > 0, roll(centre, 1), roll(beyond, -3))
-        return jnp.where(lane4 >= 2, roll(centre, 2), roll(beyond, -2))
+            low, high = roll(wide[1:], 4), roll(wide[:-1], -4)
+            x_low = roll(jnp.where(lane4 == 3, high[:-1], centre), 1)
+            x_high = roll(jnp.where(lane4 == 0, low[1:], centre), -1)
+            return x_low, x_high, low[:-1], high[1:]
+        other = jnp.where(lane_of(wide) % 4 < 2, roll(wide, -2), roll(wide, 2))
+        x_low = jnp.where(lane4 >= 2, other[1:-1], other[:-2])
+        x_high = jnp.where(lane4 < 2, other[1:-1], other[2:])
+        return x_low, x_high, roll(centre, step), roll(centre, -step)
 
     def prepare_whole(a, c, level):
         scale = 0.25**level
         step = 2**level
         for q in range(a.shape[1]):
-            low_x, low_y, low_z = get(a, 1, q), get(a, 2, q), get(a, 3, q)
-            up_x = x_next(a, 1, q, level)
-            up_y = get(a, 2, q, 0, 1)
-            up_z = jnp.where(lane >= 128 - step, 0.0, roll(low_z, -step))
-            diagonal = SHIFT * get(a, 0, q) + scale * (low_x + up_x + low_y + up_y + low_z + up_z)
-            inverse = 1.0 / diagonal
-            scaled = scale * inverse
-            c[1, q] = low_x * scaled
-            c[2, q] = up_x * scaled
-            c[3, q] = low_y * scaled
-            c[4, q] = up_y * scaled
-            c[5, q] = jnp.where(lane < step, 0.0, low_z * scaled)
-            c[6, q] = up_z * scaled
-            c[7, q] = diagonal
-            c[8, q] = inverse
-
-    def inner(ref, lead, q, value):
-        ref[lead, q, pl.ds(1, GX), pl.ds(8, 16)] = value
+            for win in HALVES:
+                low_x, low_y, low_z = get(a, 1, q, win), get(a, 2, q, win), get(a, 3, q, win)
+                up_x = x_next(get(a, 1, q, win, wide=True), level)
+                up_y = get(a, 2, q, win, 1)
+                lane = lane_of(low_z)
+                up_z = jnp.where(lane >= 128 - step, 0.0, roll(low_z, -step))
+                diagonal = SHIFT * get(a, 0, q, win) + scale * (low_x + up_x + low_y + up_y + low_z + up_z)
+                inverse = 1.0 / diagonal
+                scaled = scale * inverse
+                put_c(c, 1, q, win, low_x * scaled)
+                put_c(c, 2, q, win, up_x * scaled)
+                put_c(c, 3, q, win, low_y * scaled)
+                put_c(c, 4, q, win, up_y * scaled)
+                put_c(c, 5, q, win, jnp.where(lane < step, 0.0, low_z * scaled))
+                put_c(c, 6, q, win, up_z * scaled)
+                put_c(c, 7, q, win, diagonal)
+                put_c(c, 8, q, win, inverse)
+
+    def put_c(c, i, q, win, value):
+        x0, nx, r0, nr = win
+        c[i, q, pl.ds(x0, nx), pl.ds(r0, nr)] = value
+
+    def get_c(c, i, q, win):
+        x0, nx, r0, nr = win
+        return c[i, q, pl.ds(x0, nx), pl.ds(r0, nr)]
 
     def coarsen_whole(fine, coarse, z_step, x_step):
         for p in range(coarse.shape[1]):
-            for name in range(4):
-                value = get(fine, name, 2 * p)
-                if name != 2:
-                    value = value + get(fine, name, 2 * p + 1)
-                value = pair_first(value, z_step) if name == 3 else pair_sum(value, z_step)
-                value = pair_first(value, x_step) if name == 1 else pair_sum(value, x_step)
-                inner(coarse, name, p, value * (0.125 if name == 0 else 0.25))
-
-    def whole_residual(c, v, a, q, level):
-        step = 2**level
-        centre = get(v, a, q)
-        total = c[0, q] - centre
-        along_x = c[1, q] * x_last(v, a, q, level) + c[2, q] * x_next(v, a, q, level)
-        along_y = c[3, q] * get(v, a, q, 0, -1) + c[4, q] * get(v, a, q, 0, 1)
-        along_z = c[5, q] * roll(centre, step) + c[6, q] * roll(centre, -step)
-        return centre, total + (along_x + along_y) + along_z
-
-    def sweeps_whole(c, v, level, table, lo, hi):
+            for win in HALVES:
+                for name in range(4):
+                    value = get(fine, name, 2 * p, win)
+                    if name != 2:
+                        value = value + get(fine, name, 2 * p + 1, win)
+                    value = pair_first(value, z_step) if name == 3 else pair_sum(value, z_step)
+                    value = pair_first(value, x_step) if name == 1 else pair_sum(value, x_step)
+                    put(coarse, name, p, win, value * (0.125 if name == 0 else 0.25))
+
+    def whole_residual(c, v, a, q, win, level):
+        wide = get(v, a, q, win, wide=True)
+        centre = wide[1:-1]
+        x_low, x_high, z_low, z_high = around(wide, level)
+        along_x = get_c(c, 1, q, win) * x_low + get_c(c, 2, q, win) * x_high
+        along_y = get_c(c, 3, q, win) * get(v, a, q, win, -1) + get_c(c, 4, q, win) * get(v, a, q, win, 1)
+        along_z = get_c(c, 5, q, win) * z_low + get_c(c, 6, q, win) * z_high
+        return centre, (get_c(c, 0, q, win) - centre) + (along_x + along_y) + along_z
+
+    def sweeps_whole(c, v, level, table, lo, hi, wins):
         def body(k, carry):
             keep = choose(k, [entry[0] for entry in table])
             gain = choose(k, [entry[1] for entry in table])
             new = lax.rem(k, 2)
             old = 1 - new
             for q in range(v.shape[1]):
-                centre, r = whole_residual(c, v, old, q, level)
-                inner(v, new, q, centre + (gain * r + keep * (centre - get(v, new, q))))
+                for win in wins:
+                    centre, r = whole_residual(c, v, old, q, win, level)
+                    change = gain * r + keep * (centre - get(v, new, q, win))
+                    put(v, new, q, win, centre + change)
             return carry
 
         lax.fori_loop(lo, hi, body, 0)
 
-    def begin_whole(c, v, table, q, f):
-        g = f * c[8, q]
-        c[0, q] = g
-        inner(v, 0, q, table[0][1] * g)
-        inner(v, 1, q, jnp.zeros(shape, F32))
+    def begin_whole(c, v, table, q, win, f):
+        g = f * get_c(c, 8, q, win)
+        put_c(c, 0, q, win, g)
+        put(v, 0, q, win, table[0][1] * g)
+        put(v, 1, q, win, jnp.zeros_like(g))
 
     def down(c, v, coarse_c, coarse_v, level, coarse_table):
-        sweeps_whole(c, v, level, TABLE, 1, SWEEPS)
+        sweeps_whole(c, v, level, TABLE, 1, SWEEPS, HALVES)
         for p in range(coarse_v.shape[1]):
-            total = None
-            for q in (2 * p, 2 * p + 1):
-                _, r = whole_residual(c, v, 1, q, level)
-                r = r * c[7, q]
-                total = r if total is None else total + r
-            total = pair_sum(pair_sum(total, 2**level), level - 1) * 0.125
-            begin_whole(coarse_c, coarse_v, coarse_table, p, total)
-
-    def up(c, v, coarse_v, level):
+            for win in HALVES:
+                total = None
+                for q in (2 * p, 2 * p + 1):
+                    _, r = whole_residual(c, v, 1, q, win, level)
+                    r = r * get_c(c, 7, q, win)
+                    total = r if total is None else total + r
+                total = pair_sum(pair_sum(total, 2**level), level - 1) * 0.125
+                begin_whole(coarse_c, coarse_v, coarse_table, p, win, total)
+
+    def up(c, v, coarse_v, level, wins):
         for q in range(v.shape[1]):
-            inner(v, 1, q, get(v, 1, q) + get(coarse_v, 1, q // 2))
-        sweeps_whole(c, v, level, TABLE, 0, SWEEPS)
-
-    send_c2b(lambda copy: copy.wait_recv())
+            for win in wins:
+                put(v, 1, q, win, get(v, 1, q, win) + get(coarse_v, 1, q // 2, win))
+        sweeps_whole(c, v, level, TABLE, 0, SWEEPS, wins)
+
+    send_c2c(lambda copy: copy.wait_recv())
     for q in range(4):
         for name in range(4):
-            inner(a2, name, q, gc[:, pl.ds(8 * (q // 2) + 2 * name + q % 2, 16, stride=16)])
+            a2[name, q, pl.ds(1, GX), pl.ds(8, 16)] = gc[:, pl.ds(8 * (q // 2) + 2 * name + q % 2, 16, stride=16)]
     prepare_whole(a2, k2, 2)
     send_r2a(lambda copy: copy.wait_recv())
-    send_r2b(lambda copy: copy.start())
+    start(send_r2b)
     coarsen_whole(a2, a3, 4, 1)
     prepare_whole(a3, k3, 3)
     coarsen_whole(a3, a4, 8, 2)
     prepare_whole(a4, k4, 4)
-    send_r2b(lambda copy: copy.wait_recv())
+    arrive(send_r2b)
 
     for q in range(4):
-        begin_whole(k2, v2, TABLE, q, g2[:, pl.ds(8 * (q // 2) + q % 2, 16, stride=16)])
+        begin_whole(k2, v2, TABLE, q, (0, GX, 0, 16), g2[:, pl.ds(8 * (q // 2) + q % 2, 16, stride=16)])
     down(k2, v2, k3, v3, 2, TABLE)
     down(k3, v3, k4, v4, 3, COARSE)
-    sweeps_whole(k4, v4, 4, COARSE, 1, COARSE_SWEEPS)
-    up(k3, v3, v4, 3)
-    up(k2, v2, v3, 2)
+    sweeps_whole(k4, v4, 4, COARSE, 1, COARSE_SWEEPS, HALVES)
+    up(k3, v3, v4, 3, HALVES)
+    near_x = jnp.clip(gx - 2, 0, GX - 5)
+    near_row = jnp.clip((2 * gy + 1) // 4 - 2, 0, 8)
+    near2 = (near_x, 5, near_row, 8)
+    up(k2, v2, v3, 2, [near2])
 
     for q in range(4):
-        lin[pl.ds(1, GX), pl.ds(8 + q, 16, stride=4)] = get(v2, 1, q)
+        lin[pl.ds(1, 5), pl.ds(8 + q, 8, stride=4)] = get(v2, 1, q, near2)
     arrive(send_x1)
     lane_row = lanes((8, 128)) % 4
 
     def spread(block):
-        value = lin[gx + block, pl.ds(8 + 2 * gy - 3, 8)]
+        value = lin[gx - near_x + block, pl.ds(8 + 2 * gy - 3 - 4 * near_row, 8)]
         for x in range(4):
             one = jnp.where(lane_row == x, value, 0.0)
             one = pair_sum(pair_sum(one, 1), 2)
@@ -537,7 +579,8 @@
 
     def correct1(s):
         ok, _, _ = valid(s, 2, 8, 8, 8, 4)
-        v1[0, s + 1, pl.ds(8, 16)] = jnp.where(ok, x1[s, pl.ds(2, 16)] + pr[s // 2], 0.0)
+        v1[0, s + 1, pl.ds(8, 16)] = jnp.where(ok, x1[0, s, pl.ds(2, 16)] + pr[s // 2], 0.0)
+        c1[0, s] = jnp.where(ok, x1[1, s, pl.ds(2, 16)] * c1[8, s], 0.0)
 
     slots(2, 22, correct1)
 
@@ -577,14 +620,14 @@
 
     smooth_down(c0, v0, 1, 1, 23, finish)
 
-    for copy in send_b0 + send_c1 + send_f1 + send_x0 + send_x1:
+    for copy in send_b0 + send_c1 + send_f1 + send_x0 + send_x1 + send_r2b:
         copy.wait_send()
-    for each in (send_c2a, send_c2b, send_r2a, send_r2b):
+    for each in (send_c2a, send_c2b, send_c2c, send_r2a):
         each(lambda copy: copy.wait_send())
 
 
 def step(right_side, alpha, beta_x, beta_y, beta_z):
-    copies = 8 + 14 + 14 + 8 + 14 + 2 * (GX - 1 + GY - 1)
+    copies = 8 + 14 + 8 + 8 + 14 + 2 * (GX - 1 + GY - 1)
     vmem = [
         (5, 25, 24, 128),
         (9, 24, 16, 128),
@@ -594,12 +637,12 @@
         (5, 25, 24, 128),
         (9, 24, 16, 128),
         (2, 26, 32, 128),
-        (24, 24, 128),
+        (2, 24, 24, 128),
         (12, 8, 128),
         (12, 16, 128),
         (GX, 8 * GY, 128),
         (GX, 8 * GY, 128),
-        (GX + 2, 80, 128),
+        (7, 48, 128),
     ]
     for planes in (4, 2, 1):
         vmem += [(4, planes, GX + 2, 32, 128), (9, planes, GX, 16, 128), (2, planes, GX + 2, 32, 128)]
@@ -615,7 +658,7 @@
             pltpu.SemaphoreType.DMA((copies,)),
         ],
         compiler_params=pltpu.CompilerParams(
-            collective_id=0, has_side_effects=True, vmem_limit_bytes=48 * 1024 * 1024
+            collective_id=0, has_side_effects=True, vmem_limit_bytes=60 * 1024 * 1024
         ),
         name="vcycle",
     )(right_side, alpha, beta_x, beta_y, beta_z)

time: 71.9 us -> 58.2 us (0.81)
  Pallas kernels: 66.8 us -> 56.6 us
  local copies, waits for them, and re-layouts: 4.83 us -> 1.47 us
    pallas_call x1, Pallas kernels: 66.8 us -> 56.6 us  [step(): pl.pallas_call(kernel, out_shape=jax.ShapeDtypeStruct((16, 8, 128), F32),...]
    unnamed x11 -> x1, local copies, waits for them, and re-layouts: 4.83 us -> 1.47 us
where the time goes in v2:
time: 58.2 us; the launch traced here: 58.1 us
  Pallas kernels  56.6 us (97%)
  local copies, waits for them, and re-layouts  1.47 us (3%)
    pallas_call x1, Pallas kernels, step(): pl.pallas_call(kernel, out_shape=jax.ShapeDtypeStruct((16, 8, 128), F32),...  56.6 us
    unnamed x1, local copies, waits for them, and re-layouts  1.47 us

profile of v2, /device:TPU:1, one launch (start us, length us, event | category | flops | bytes accessed | tf_op | source)
XLA Modules:
  0.0 58.1 jit_solution(14069712990818476967)
XLA Ops:
  0.0 56.6 %vcycle.1 = f32[16,8,128]{2,1,0:T(8,128)} custom-call(f32[16,8,128]{2,1,0:T(8,128)} %f_in.1, f32[16,8,128]{2,1,0:T(8,128)} %al_in.1, f32[16,8,128]{2,1,0:T(8,128)} %bx_in.1, f32[16,8,128]{2,1,0:T(8,128)} %by_in.1, f32[16,8,128]{2,1,0:T(8,128)} %bz_in.1), custom_call_target="tpu_custom_call" | custom-call | tf_op jit(solution)/shard_map/vcycle/pallas_call | solution.py:649
  56.6 1.5 %copy.7 = f32[16,8,128]{2,1,0:T(8,128)} copy(f32[16,8,128]{2,1,0:T(8,128)} %vcycle.1) | data formatting | bytes 131072

commit v3 on v2

--- a/solution.py
+++ b/solution.py
@@ -70,19 +70,13 @@
     return jnp.where((lane // step) % 2 == 0, value, roll(value, step))
 
 
-def choose(index, values):
-    out = jnp.float32(values[-1])
-    for i in range(len(values) - 2, -1, -1):
-        out = jnp.where(index == i, jnp.float32(values[i]), out)
-    return out
-
-
 def kernel(
     f_in, al_in, bx_in, by_in, bz_in, out,
-    b0, c0, v0, x0, t0, b1, c1, v1, x1, t1, pr,
-    gc, g2, lin, a2, k2, v2, a3, k3, v3, a4, k4, v4,
+    b0, c0, w0, v0a, v0b, x0, t0, b1, c1, w1, v1a, v1b, x1, t1, pr,
+    gc, g2, turn, lin, a2, k2, w2, v2a, v2b, a3, k3, a4, k4,
     in_sem, ss, rs,
 ):
+    v0, v1 = (v0a, v0b), (v1a, v1b)
     gx = lax.axis_index("gx")
     gy = lax.axis_index("gy")
     counter = [0]
@@ -210,19 +204,6 @@
     for dx, dy in diagonal:
         greet(near(dx, dy))
 
-    edge = jnp.zeros((32, 128), F32)
-    side = jnp.zeros((GX, 8, 128), F32)
-    for ref in (a2, a3, a4, v2, v3, v4):
-
-        def clear(i, carry, ref=ref):
-            p, q = i // ref.shape[1], i % ref.shape[1]
-            ref[p, q, 0] = edge
-            ref[p, q, GX + 1] = edge
-            ref[p, q, 1 : GX + 1, 0:8] = side
-            ref[p, q, 1 : GX + 1, 24:32] = side
-            return carry
-
-        lax.fori_loop(0, ref.shape[0] * ref.shape[1], clear, 0)
     for copy in inputs:
         copy.wait()
 
@@ -309,55 +290,55 @@
 
         slots(lo, hi, body)
 
-    def scaled_residual(c, v, a, s, step, rows=16, off=0):
+    def scaled_residual(c, w, v, s, step, rows=16, off=0):
         at = pl.ds(8 + off, rows)
-        centre = v[a, s + 1, at]
+        centre = v[s + 1, at]
         k = pl.ds(off, rows)
-        total = c[0, s, k] - centre
-        along_x = c[1, s, k] * v[a, s, at] + c[2, s, k] * v[a, s + 2, at]
-        along_y = c[3, s, k] * v[a, s + 1, pl.ds(7 + off, rows)] + c[4, s, k] * v[a, s + 1, pl.ds(9 + off, rows)]
+        total = w[s, k] - centre
+        along_x = c[1, s, k] * v[s, at] + c[2, s, k] * v[s + 2, at]
+        along_y = c[3, s, k] * v[s + 1, pl.ds(7 + off, rows)] + c[4, s, k] * v[s + 1, pl.ds(9 + off, rows)]
         along_z = c[5, s, k] * roll(centre, step) + c[6, s, k] * roll(centre, -step)
         return centre, total + (along_x + along_y) + along_z
 
-    def sweep(c, v, a, s, step, k, first):
+    def sweep(c, w, v, a, s, step, k, first, rows=16, off=0):
         keep, gain = TABLE[k]
-        centre, r = scaled_residual(c, v, a, s, step)
+        centre, r = scaled_residual(c, w, v[a], s, step, rows, off)
         change = gain * r
         if not first:
-            change = change + keep * (centre - v[1 - a, s + 1, pl.ds(8, 16)])
+            change = change + keep * (centre - v[1 - a][s + 1, pl.ds(8 + off, rows)])
         return centre + change
 
-    def smooth_up(b, c, v, row, step, lo, hi):
+    def smooth_up(b, c, w, v, row, step, lo, hi, rows, off):
         def begin(s):
             g = b[0, s, pl.ds(row, 16)] * c[8, s]
-            c[0, s] = g
-            v[0, s + 1, pl.ds(8, 16)] = TABLE[0][1] * g
+            w[s] = g
+            v[0][s + 1, pl.ds(8, 16)] = TABLE[0][1] * g
 
         slots(lo, hi, begin)
 
         def second(s):
             keep, gain = TABLE[1]
-            centre, r = scaled_residual(c, v, 0, s, step)
-            v[1, s + 1, pl.ds(8, 16)] = centre + gain * r + keep * centre
+            centre, r = scaled_residual(c, w, v[0], s, step)
+            v[1][s + 1, pl.ds(8, 16)] = centre + gain * r + keep * centre
 
         slots(lo + 1, hi - 1, second)
         for k in (2, 3):
             a = (k - 1) % 2
 
             def body(s, k=k, a=a):
-                v[1 - a, s + 1, pl.ds(8, 16)] = sweep(c, v, a, s, step, k, False)
+                v[1 - a][s + 1, pl.ds(8 + off, rows)] = sweep(c, w, v, a, s, step, k, False, rows, off)
 
             slots(lo + k, hi - k, body)
 
     arrive(send_b0)
     prepare(b0, c0, 0, 1.0, 1, 16, 8, 4, 0, 24)
-    smooth_up(b0, c0, v0, 0, 1, 0, 24)
+    smooth_up(b0, c0, w0, v0, 0, 1, 0, 24, 16, 0)
 
     def resid0(i):
         total = None
         for j in range(2):
             s = 4 + 2 * i + j
-            centre, r = scaled_residual(c0, v0, 1, s, 1, 8, 4)
+            centre, r = scaled_residual(c0, w0, v0[1], s, 1, 8, 4)
             x0[s, 4:12] = centre
             r = r * c0[7, s, 4:12]
             total = r if total is None else total + r
@@ -385,13 +366,13 @@
     lax.fori_loop(1, GY // 2 + 1, forward, 0)
     arrive(send_f1)
 
-    smooth_up(b1, c1, v1, 2, 2, 4, 20)
+    smooth_up(b1, c1, w1, v1, 2, 2, 4, 20, 8, 4)
 
     def resid1(i):
         total = None
         for j in range(2):
             s = 8 + 2 * i + j
-            centre, r = scaled_residual(c1, v1, 1, s, 2, 4, 6)
+            centre, r = scaled_residual(c1, w1, v1[1], s, 2, 4, 6)
             x1[0, s, 8:12] = centre
             r = r * c1[7, s, 6:10]
             total = r if total is None else total + r
@@ -403,172 +384,206 @@
     send_r2a(lambda copy: copy.start())
     start(send_x1)
 
-    HALVES = [(0, GX, 0, 8), (0, GX, 8, 8)]
-
-    def lane_of(value):
-        return lanes(value.shape)
-
-    def get(ref, lead, q, win, dy=0, wide=False):
-        planes = ref.shape[1]
-        row = 8
-        if q + dy >= planes:
-            q, row = 0, 9
-        elif q + dy < 0:
-            q, row = planes - 1, 7
-        else:
-            q = q + dy
-        x0, nx, r0, nr = win
-        start, count = (x0, nx + 2) if wide else (x0 + 1, nx)
-        return ref[lead, q, pl.ds(start, count), pl.ds(row + r0, nr)]
-
-    def put(ref, lead, q, win, value):
-        x0, nx, r0, nr = win
-        ref[lead, q, pl.ds(x0 + 1, nx), pl.ds(8 + r0, nr)] = value
-
-    def x_next(wide, level):
-        if level == 4:
-            return wide[2:]
-        lane4 = lane_of(wide[1:-1]) % 4
-        if level == 2:
-            return roll(jnp.where(lane4 == 0, roll(wide[2:], 4), wide[1:-1]), -1)
-        return jnp.where(lane4 < 2, roll(wide[1:-1], -2), roll(wide[2:], 2))
-
-    def around(wide, level):
-        step = 2**level
-        centre = wide[1:-1]
-        lane4 = lane_of(centre) % 4
-        if level == 4:
-            return wide[:-2], wide[2:], roll(centre, step), roll(centre, -step)
-        if level == 2:
-            low, high = roll(wide[1:], 4), roll(wide[:-1], -4)
-            x_low = roll(jnp.where(lane4 == 3, high[:-1], centre), 1)
-            x_high = roll(jnp.where(lane4 == 0, low[1:], centre), -1)
-            return x_low, x_high, low[:-1], high[1:]
-        other = jnp.where(lane_of(wide) % 4 < 2, roll(wide, -2), roll(wide, 2))
-        x_low = jnp.where(lane4 >= 2, other[1:-1], other[:-2])
-        x_high = jnp.where(lane4 < 2, other[1:-1], other[2:])
-        return x_low, x_high, roll(centre, step), roll(centre, -step)
+    tile = (1, 8, 128)
+    sub = lax.broadcasted_iota(jnp.int32, tile, 1)
+    lane = lanes(tile)
+    ENDS = {"x": (lane // 16 == 0, lane // 16 == 7), "y": (lane % 16 == 0, lane % 16 == 15), "z": (sub == 0, sub == 7)}
+
+    def turned(value, shift):
+        return pltpu.roll(value, shift % 8, 1)
+
+    def high(get, n, j, k, axis):
+        if axis == "x":
+            value = get(j, k)
+            last = roll(value[:1], -16)
+            return last if n == 1 else jnp.concatenate([value[1:], last], axis=0)
+        if axis == "y":
+            return get(j + 1, k) if j + 1 < n else roll(get(0, k), -1)
+        return get(j, k + 1) if k + 1 < n else turned(get(j, 0), -1)
+
+    def low(get, n, j, k, axis):
+        if axis == "x":
+            value = get(j, k)
+            first = roll(value[n - 1 :], 16)
+            return first if n == 1 else jnp.concatenate([first, value[: n - 1]], axis=0)
+        if axis == "y":
+            return get(j - 1, k) if j > 0 else roll(get(n - 1, k), 1)
+        return get(j, k - 1) if k > 0 else turned(get(j, n - 1), 1)
+
+    def without(value, n, j, k, axis, end):
+        edge = (n - 1) * end
+        mask = ENDS[axis][end]
+        if axis == "x":
+            parts = [value[i : i + 1] for i in range(n)]
+            parts[edge] = jnp.where(mask, 0.0, parts[edge])
+            return parts[0] if n == 1 else jnp.concatenate(parts, axis=0)
+        if (j if axis == "y" else k) != edge:
+            return value
+        return jnp.where(mask, 0.0, value)
+
+    def blocks(n):
+        return [(j, k) for j in range(n) for k in range(n)]
 
     def prepare_whole(a, c, level):
         scale = 0.25**level
-        step = 2**level
-        for q in range(a.shape[1]):
-            for win in HALVES:
-                low_x, low_y, low_z = get(a, 1, q, win), get(a, 2, q, win), get(a, 3, q, win)
-                up_x = x_next(get(a, 1, q, win, wide=True), level)
-                up_y = get(a, 2, q, win, 1)
-                lane = lane_of(low_z)
-                up_z = jnp.where(lane >= 128 - step, 0.0, roll(low_z, -step))
-                diagonal = SHIFT * get(a, 0, q, win) + scale * (low_x + up_x + low_y + up_y + low_z + up_z)
-                inverse = 1.0 / diagonal
-                scaled = scale * inverse
-                put_c(c, 1, q, win, low_x * scaled)
-                put_c(c, 2, q, win, up_x * scaled)
-                put_c(c, 3, q, win, low_y * scaled)
-                put_c(c, 4, q, win, up_y * scaled)
-                put_c(c, 5, q, win, jnp.where(lane < step, 0.0, low_z * scaled))
-                put_c(c, 6, q, win, up_z * scaled)
-                put_c(c, 7, q, win, diagonal)
-                put_c(c, 8, q, win, inverse)
-
-    def put_c(c, i, q, win, value):
-        x0, nx, r0, nr = win
-        c[i, q, pl.ds(x0, nx), pl.ds(r0, nr)] = value
-
-    def get_c(c, i, q, win):
-        x0, nx, r0, nr = win
-        return c[i, q, pl.ds(x0, nx), pl.ds(r0, nr)]
-
-    def coarsen_whole(fine, coarse, z_step, x_step):
-        for p in range(coarse.shape[1]):
-            for win in HALVES:
-                for name in range(4):
-                    value = get(fine, name, 2 * p, win)
-                    if name != 2:
-                        value = value + get(fine, name, 2 * p + 1, win)
-                    value = pair_first(value, z_step) if name == 3 else pair_sum(value, z_step)
-                    value = pair_first(value, x_step) if name == 1 else pair_sum(value, x_step)
-                    put(coarse, name, p, win, value * (0.125 if name == 0 else 0.25))
-
-    def whole_residual(c, v, a, q, win, level):
-        wide = get(v, a, q, win, wide=True)
-        centre = wide[1:-1]
-        x_low, x_high, z_low, z_high = around(wide, level)
-        along_x = get_c(c, 1, q, win) * x_low + get_c(c, 2, q, win) * x_high
-        along_y = get_c(c, 3, q, win) * get(v, a, q, win, -1) + get_c(c, 4, q, win) * get(v, a, q, win, 1)
-        along_z = get_c(c, 5, q, win) * z_low + get_c(c, 6, q, win) * z_high
-        return centre, (get_c(c, 0, q, win) - centre) + (along_x + along_y) + along_z
-
-    def sweeps_whole(c, v, level, table, lo, hi, wins):
-        def body(k, carry):
-            keep = choose(k, [entry[0] for entry in table])
-            gain = choose(k, [entry[1] for entry in table])
-            new = lax.rem(k, 2)
-            old = 1 - new
-            for q in range(v.shape[1]):
-                for win in wins:
-                    centre, r = whole_residual(c, v, old, q, win, level)
-                    change = gain * r + keep * (centre - get(v, new, q, win))
-                    put(v, new, q, win, centre + change)
-            return carry
-
-        lax.fori_loop(lo, hi, body, 0)
-
-    def begin_whole(c, v, table, q, win, f):
-        g = f * get_c(c, 8, q, win)
-        put_c(c, 0, q, win, g)
-        put(v, 0, q, win, table[0][1] * g)
-        put(v, 1, q, win, jnp.zeros_like(g))
-
-    def down(c, v, coarse_c, coarse_v, level, coarse_table):
-        sweeps_whole(c, v, level, TABLE, 1, SWEEPS, HALVES)
-        for p in range(coarse_v.shape[1]):
-            for win in HALVES:
-                total = None
-                for q in (2 * p, 2 * p + 1):
-                    _, r = whole_residual(c, v, 1, q, win, level)
-                    r = r * get_c(c, 7, q, win)
-                    total = r if total is None else total + r
-                total = pair_sum(pair_sum(total, 2**level), level - 1) * 0.125
-                begin_whole(coarse_c, coarse_v, coarse_table, p, win, total)
-
-    def up(c, v, coarse_v, level, wins):
-        for q in range(v.shape[1]):
-            for win in wins:
-                put(v, 1, q, win, get(v, 1, q, win) + get(coarse_v, 1, q // 2, win))
-        sweeps_whole(c, v, level, TABLE, 0, SWEEPS, wins)
+        n = a.shape[1]
+        for j, k in blocks(n):
+            diagonal = SHIFT * a[0, j, k]
+            faces = []
+            for i, axis in enumerate("xyz"):
+                below = a[1 + i, j, k]
+                above = high(lambda j, k, i=i: a[1 + i, j, k], n, j, k, axis)
+                above = without(above, n, j, k, axis, 1)
+                faces.append((without(below, n, j, k, axis, 0), above))
+                diagonal = diagonal + scale * (below + above)
+            inverse = 1.0 / diagonal
+            scaled = scale * inverse
+            for i, (below, above) in enumerate(faces):
+                c[1 + 2 * i, j, k] = below * scaled
+                c[2 + 2 * i, j, k] = above * scaled
+            c[7, j, k] = diagonal
+            c[8, j, k] = inverse
+
+    def coarser(take, n, j, k, skip=""):
+        total = None
+        for fine_j in (2 * j, 2 * j + 1)[: 1 if skip == "y" else 2]:
+            for fine_k in (2 * k, 2 * k + 1)[: 1 if skip == "z" else 2]:
+                value = take(fine_j, fine_k)
+                total = value if total is None else total + value
+        pairs = total.reshape(n // 2, 2, 8, 128)
+        return pairs[:, 0] if skip == "x" else pairs[:, 0] + pairs[:, 1]
+
+    def coarsen_whole(fine, coarse):
+        n = fine.shape[1]
+        for j, k in blocks(n // 2):
+            for i, skip in enumerate(("", "x", "y", "z")):
+                value = coarser(lambda j, k, i=i: fine[i, j, k], n, j, k, skip)
+                coarse[i, j, k] = value * (0.25 if skip else 0.125)
+
+    def whole_residual(c, w, get, n, j, k):
+        centre = get(j, k)
+        parts = []
+        for i, axis in enumerate("xyz"):
+            parts.append(c[1 + 2 * i, j, k] * low(get, n, j, k, axis) + c[2 + 2 * i, j, k] * high(get, n, j, k, axis))
+        return centre, (w(j, k) - centre) + (parts[0] + parts[1]) + parts[2]
+
+    class InRefs:
+        def __init__(self, ref):
+            self.ref = ref
+
+        def __call__(self, j, k):
+            return self.ref[j, k]
+
+        def put(self, j, k, value):
+            self.ref[j, k] = value
+
+    class InValues:
+        def __init__(self):
+            self.values = {}
+
+        def __call__(self, j, k):
+            return self.values[j, k]
+
+        def put(self, j, k, value):
+            self.values[j, k] = value
+
+    def sweeps_whole(c, w, old, new, n, table, lo, hi):
+        for sweep_index in range(lo, hi):
+            keep, gain = table[sweep_index]
+            results = []
+            for j, k in blocks(n):
+                centre, r = whole_residual(c, w, old, n, j, k)
+                change = gain * r
+                if sweep_index == 1 and lo == 1:
+                    change = change + keep * centre
+                elif sweep_index:
+                    change = change + keep * (centre - new(j, k))
+                if isinstance(new, InRefs):
+                    new.put(j, k, centre + change)
+                else:
+                    results.append((j, k, centre + change))
+            if results:
+                new = InValues()
+                for j, k, value in results:
+                    new.put(j, k, value)
+            old, new = new, old
+        return old, new
+
+    def start_whole(c, w, v, n, table, f):
+        for j, k in blocks(n):
+            g = f(j, k) * c[8, j, k]
+            w.put(j, k, g)
+            v.put(j, k, table[0][1] * g)
+
+    def restricted(c, w, v, n):
+        result = InValues()
+        scaled = InValues()
+        for j, k in blocks(n):
+            _, r = whole_residual(c, w, v, n, j, k)
+            scaled.put(j, k, r * c[7, j, k])
+        for j, k in blocks(n // 2):
+            result.put(j, k, coarser(scaled, n, j, k) * 0.125)
+        return result
+
+    def corrected(v, coarse, n, into):
+        for j, k in blocks(n):
+            value = coarse(j // 2, k // 2)
+            value = jnp.broadcast_to(value[:, None], (n // 2, 2, 8, 128)).reshape(n, 8, 128)
+            into.put(j, k, v(j, k) + value)
 
     send_c2c(lambda copy: copy.wait_recv())
-    for q in range(4):
+    for j in range(4):
         for name in range(4):
-            a2[name, q, pl.ds(1, GX), pl.ds(8, 16)] = gc[:, pl.ds(8 * (q // 2) + 2 * name + q % 2, 16, stride=16)]
+            rows = gc[:, pl.ds(8 * (j // 2) + 2 * name + j % 2, 16, stride=16)]
+            turn[name, j] = rows.reshape(128, 128).T
+    for j in range(4):
+        for name in range(4):
+            for k in range(4):
+                for i in range(4):
+                    a2[name, j, k, i] = turn[name, j, pl.ds(4 * k + i, 8, stride=16)]
     prepare_whole(a2, k2, 2)
     send_r2a(lambda copy: copy.wait_recv())
     start(send_r2b)
-    coarsen_whole(a2, a3, 4, 1)
+    coarsen_whole(a2, a3)
     prepare_whole(a3, k3, 3)
-    coarsen_whole(a3, a4, 8, 2)
+    coarsen_whole(a3, a4)
     prepare_whole(a4, k4, 4)
     arrive(send_r2b)
 
-    for q in range(4):
-        begin_whole(k2, v2, TABLE, q, (0, GX, 0, 16), g2[:, pl.ds(8 * (q // 2) + q % 2, 16, stride=16)])
-    down(k2, v2, k3, v3, 2, TABLE)
-    down(k3, v3, k4, v4, 3, COARSE)
-    sweeps_whole(k4, v4, 4, COARSE, 1, COARSE_SWEEPS, HALVES)
-    up(k3, v3, v4, 3, HALVES)
-    near_x = jnp.clip(gx - 2, 0, GX - 5)
-    near_row = jnp.clip((2 * gy + 1) // 4 - 2, 0, 8)
-    near2 = (near_x, 5, near_row, 8)
-    up(k2, v2, v3, 2, [near2])
-
-    for q in range(4):
-        lin[pl.ds(1, 5), pl.ds(8 + q, 8, stride=4)] = get(v2, 1, q, near2)
+    for j in range(4):
+        rows = g2[:, pl.ds(8 * (j // 2) + j % 2, 16, stride=16)]
+        turn[4, j] = rows.reshape(128, 128).T
+
+    def f2(j, k):
+        return jnp.stack([turn[4, j, pl.ds(4 * k + i, 8, stride=16)] for i in range(4)])
+
+    field2, before2, source2 = InRefs(v2a), InRefs(v2b), InRefs(w2)
+    start_whole(k2, source2, field2, 4, TABLE, f2)
+    field2, before2 = sweeps_whole(k2, source2, field2, before2, 4, TABLE, 1, SWEEPS)
+    field3, source3 = InValues(), InValues()
+    start_whole(k3, source3, field3, 2, TABLE, restricted(k2, source2, field2, 4))
+    field3, _ = sweeps_whole(k3, source3, field3, InValues(), 2, TABLE, 1, SWEEPS)
+    field4, source4 = InValues(), InValues()
+    start_whole(k4, source4, field4, 1, COARSE, restricted(k3, source3, field3, 2))
+    field4, _ = sweeps_whole(k4, source4, field4, InValues(), 1, COARSE, 1, COARSE_SWEEPS)
+    next3 = InValues()
+    corrected(field3, field4, 2, next3)
+    field3, _ = sweeps_whole(k3, source3, next3, InValues(), 2, TABLE, 0, SWEEPS)
+    corrected(field2, field3, 4, field2)
+    field2, _ = sweeps_whole(k2, source2, field2, before2, 4, TABLE, 0, SWEEPS)
+
+    for j in range(4):
+        for k in range(4):
+            value = field2(j, k)
+            for i in range(4):
+                turn[4, j, pl.ds(4 * k + i, 8, stride=16)] = value[i]
+    for j in range(4):
+        lin[pl.ds(1, GX), pl.ds(8 + j, 16, stride=4)] = turn[4, j].T.reshape(GX, 16, 128)
     arrive(send_x1)
     lane_row = lanes((8, 128)) % 4
 
     def spread(block):
-        value = lin[gx - near_x + block, pl.ds(8 + 2 * gy - 3 - 4 * near_row, 8)]
+        value = lin[gx + block, pl.ds(8 + 2 * gy - 3, 8)]
         for x in range(4):
             one = jnp.where(lane_row == x, value, 0.0)
             one = pair_sum(pair_sum(one, 1), 2)
@@ -579,28 +594,28 @@
 
     def correct1(s):
         ok, _, _ = valid(s, 2, 8, 8, 8, 4)
-        v1[0, s + 1, pl.ds(8, 16)] = jnp.where(ok, x1[0, s, pl.ds(2, 16)] + pr[s // 2], 0.0)
-        c1[0, s] = jnp.where(ok, x1[1, s, pl.ds(2, 16)] * c1[8, s], 0.0)
+        v1[0][s + 1, pl.ds(8, 16)] = jnp.where(ok, x1[0, s, pl.ds(2, 16)] + pr[s // 2], 0.0)
+        w1[s] = jnp.where(ok, x1[1, s, pl.ds(2, 16)] * c1[8, s], 0.0)
 
     slots(2, 22, correct1)
 
-    def smooth_down(c, v, step, lo, hi, last):
+    def smooth_down(c, w, v, step, lo, hi, last):
         for k in range(SWEEPS):
             a = k % 2
 
             def body(s, k=k, a=a):
-                value = sweep(c, v, a, s, step, k, k == 0)
                 if k == SWEEPS - 1:
-                    last(s, value)
-                else:
-                    v[1 - a, s + 1, pl.ds(8, 16)] = value
+                    last(s, sweep(c, w, v, a, s, step, k, False, 8, 4))
+                    return
+                value = sweep(c, w, v, a, s, step, k, k == 0)
+                v[1 - a][s + 1, pl.ds(8, 16)] = value
 
             slots(lo + k, hi - k, body)
 
     def spread0(s, value):
-        t1[s - 6] = value[4:12]
-
-    smooth_down(c1, v1, 2, 3, 21, spread0)
+        t1[s - 6] = value
+
+    smooth_down(c1, w1, v1, 2, 3, 21, spread0)
 
     def widen(i):
         pr[i, pl.ds(0, 8, stride=2)] = t1[i]
@@ -611,14 +626,14 @@
 
     def correct0(s):
         ok, _, _ = valid(s, 0, 4, 16, 4, 8)
-        v0[0, s + 1, pl.ds(8, 16)] = jnp.where(ok, x0[s] + pr[s // 2], 0.0)
+        v0[0][s + 1, pl.ds(8, 16)] = jnp.where(ok, x0[s] + pr[s // 2], 0.0)
 
     slots(0, 24, correct0)
 
     def finish(s, value):
-        out[s - 4] = value[4:12]
-
-    smooth_down(c0, v0, 1, 1, 23, finish)
+        out[s - 4] = value
+
+    smooth_down(c0, w0, v0, 1, 1, 23, finish)
 
     for copy in send_b0 + send_c1 + send_f1 + send_x0 + send_x1 + send_r2b:
         copy.wait_send()
@@ -631,21 +646,28 @@
     vmem = [
         (5, 25, 24, 128),
         (9, 24, 16, 128),
-        (2, 26, 32, 128),
+        (24, 16, 128),
+        (26, 32, 128),
+        (26, 32, 128),
         (24, 16, 128),
         (8, 8, 128),
         (5, 25, 24, 128),
         (9, 24, 16, 128),
-        (2, 26, 32, 128),
+        (24, 16, 128),
+        (26, 32, 128),
+        (26, 32, 128),
         (2, 24, 24, 128),
         (12, 8, 128),
         (12, 16, 128),
         (GX, 8 * GY, 128),
         (GX, 8 * GY, 128),
-        (7, 48, 128),
+        (5, 4, 128, 128),
+        (GX + 2, 80, 128),
     ]
-    for planes in (4, 2, 1):
-        vmem += [(4, planes, GX + 2, 32, 128), (9, planes, GX, 16, 128), (2, planes, GX + 2, 32, 128)]
+    for n in (4, 2, 1):
+        vmem += [(4, n, n, n, 8, 128), (9, n, n, n, 8, 128)]
+        if n == 4:
+            vmem += [(n, n, n, 8, 128)] * 3
     return pl.pallas_call(
         kernel,
         out_shape=jax.ShapeDtypeStruct((16, 8, 128), F32),

time: 58.2 us -> 52 us (0.89)
  Pallas kernels: 56.6 us -> 50.4 us
    pallas_call x1, Pallas kernels: 56.6 us -> 50.4 us  [step(): pl.pallas_call(kernel, out_shape=jax.ShapeDtypeStruct((16, 8, 128), F32),...]
where the time goes in v3:
time: 52 us; the launch traced here: 51.9 us
  Pallas kernels  50.4 us (97%)
  local copies, waits for them, and re-layouts  1.47 us (3%)
    pallas_call x1, Pallas kernels, step(): pl.pallas_call(kernel, out_shape=jax.ShapeDtypeStruct((16, 8, 128), F32),...  50.4 us
    unnamed x1, local copies, waits for them, and re-layouts  1.47 us

profile of v3, /device:TPU:1, one launch (start us, length us, event | category | flops | bytes accessed | tf_op | source)
XLA Modules:
  0.0 51.9 jit_solution(4852036567517318654)
XLA Ops:
  0.0 50.4 %vcycle.1 = f32[16,8,128]{2,1,0:T(8,128)} custom-call(f32[16,8,128]{2,1,0:T(8,128)} %f_in.1, f32[16,8,128]{2,1,0:T(8,128)} %al_in.1, f32[16,8,128]{2,1,0:T(8,128)} %bx_in.1, f32[16,8,128]{2,1,0:T(8,128)} %by_in.1, f32[16,8,128]{2,1,0:T(8,128)} %bz_in.1), custom_call_target="tpu_custom_call" | custom-call | tf_op jit(solution)/shard_map/vcycle/pallas_call | solution.py:671
  50.4 1.5 %copy.7 = f32[16,8,128]{2,1,0:T(8,128)} copy(f32[16,8,128]{2,1,0:T(8,128)} %vcycle.1) | data formatting | bytes 131072

commit v4 on v3

--- a/solution.py
+++ b/solution.py
@@ -18,6 +18,12 @@
 COARSE_SWEEPS = 12
 GX = 8
 GY = 32
+CHUNK = 4
+FAR_FIRST = [4, 3, 5, 2, 6, 1, 7]
+LINE = sorted(
+    [(a, b, e) for a in range(4) for b in range(4) for e in range(2) if a + b + e],
+    key=lambda t: -(2 * min(t[0], 4 - t[0]) + 2 * min(t[1], 4 - t[1]) + t[2]),
+)
 
 
 def chebyshev_table(count, lower, upper):
@@ -142,8 +148,9 @@
         rows = pl.ds(pl.multiple_of(8 * lax.rem(gy - 2 * (i - 1) + GY, GY), 8), 8)
         return remote(gc.at[:, rows], gc.at[:, rows], s, (gx, gy + 1 - 2 * lax.rem(gy, 2)))
 
-    def r2_gx(i, s):
-        return remote(g2.at[gx, own_rows(2)], g2.at[gx, own_rows(2)], s, gx_peer(i))
+    def r2_gx(i):
+        counter[0] += 1
+        return remote(g2.at[gx, own_rows(2)], g2.at[gx, own_rows(2)], counter[0] - 1, gx_peer(i))
 
     send_b0 = halo(
         lambda x, y: b0.at[:, x, y], NEAR, 4, 16, 4, 8,
@@ -169,15 +176,15 @@
     c2b_base = counter[0]
     send_c2b = many(GY // 2 - 1, c2_gy)
     send_c2c = many(GY // 2, c2_core)
-    send_r2a = many(GX - 1, r2_gx)
+    send_r2a = [r2_gx(i) for i in FAR_FIRST]
+    along_x = [8 * lax.rem(gy // 8 + a, 4) for a in range(4)]
+    along_y = [2 * lax.rem(gy // 2 + b, 4) for b in range(4)]
+    core = [lax.rem(gy + e, 2) for e in range(2)]
+    line = [(gx, along_x[a] + along_y[b] + core[e]) for a, b, e in LINE]
     send_r2b = []
-    for a, b, e in sorted(
-        [(a, b, e) for a in range(4) for b in range(4) for e in range(2) if a + b + e],
-        key=lambda t: -(2 * min(t[0], 4 - t[0]) + 2 * min(t[1], 4 - t[1]) + t[2]),
-    ):
-        x, y, core = lax.rem(gy // 8 + a, 4), lax.rem(gy // 2 + b, 4), lax.rem(gy + e, 2)
+    for device in line:
         own = g2.at[:, own_rows(2)]
-        send_r2b.append(remote(own, own, counter[0], (gx, 8 * x + 2 * y + core)))
+        send_r2b.append(remote(own, own, counter[0], device))
         counter[0] += 1
 
     inputs = [
@@ -190,19 +197,15 @@
     def greet(device):
         pl.semaphore_signal(barrier, inc=1, device_id=device, device_id_type=MESH)
 
-    def greet_gx(i, carry):
+    diagonal = [side for side in NEAR + FAR_XY if side[0] and side[1]]
+    for device in line[:18]:
+        greet(device)
+    for i in FAR_FIRST:
         greet(gx_peer(i))
-        return carry
-
-    def greet_gy(i, carry):
-        greet(gy_peer(i))
-        return carry
-
-    diagonal = [side for side in NEAR + FAR_XY if side[0] and side[1]]
-    lax.fori_loop(1, GX, greet_gx, 0)
-    lax.fori_loop(1, GY, greet_gy, 0)
     for dx, dy in diagonal:
         greet(near(dx, dy))
+    for device in line[18:]:
+        greet(device)
 
     for copy in inputs:
         copy.wait()
@@ -255,49 +258,58 @@
     send_c2b(lambda copy: copy.start())
 
     def valid(s, rows, off_x, n_x, off_y, n_y):
-        x = gx * n_x + s - off_x
-        y = gy * n_y + lax.broadcasted_iota(jnp.int32, (16, 128), 0) + rows - off_y
+        shape = (CHUNK, 16, 128)
+        x = gx * n_x + s - off_x + lax.broadcasted_iota(jnp.int32, shape, 0)
+        y = gy * n_y + rows - off_y + lax.broadcasted_iota(jnp.int32, shape, 1)
         inside = jnp.logical_and(y >= 0, y < GY * n_y)
         return jnp.logical_and(inside, jnp.logical_and(x >= 0, x < GX * n_x)), x, y
 
-    def slots(lo, hi, body, unroll=4):
-        def run(s, carry):
-            body(s)
+    def slots(lo, hi, body):
+        runs = -(-(hi - lo) // CHUNK)
+        first = lo - (runs * CHUNK - (hi - lo)) // 2
+
+        def run(i, carry):
+            body(first + CHUNK * i)
             return carry
 
-        lax.fori_loop(lo, hi, run, 0, unroll=unroll)
+        lax.fori_loop(0, runs, run, 0, unroll=2)
+
+    def some(s):
+        return pl.ds(s, CHUNK)
 
     def prepare(b, c, row, scale, step, n_x, n_y, off, lo, hi):
-        lane = lanes((16, 128))
-
         def body(s):
+            at = pl.ds(row, 16)
             ok, x, y = valid(s, row, off, n_x, off, n_y)
-            low_x, low_y, low_z = b[2, s, pl.ds(row, 16)], b[3, s, pl.ds(row, 16)], b[4, s, pl.ds(row, 16)]
-            up_x = jnp.where(x + 1 < GX * n_x, b[2, s + 1, pl.ds(row, 16)], 0.0)
-            up_y = jnp.where(y + 1 < GY * n_y, b[3, s, pl.ds(row + 1, 16)], 0.0)
+            lane = lanes(ok.shape)
+            low_x, low_y, low_z = b[2, some(s), at], b[3, some(s), at], b[4, some(s), at]
+            up_x = jnp.where(x + 1 < GX * n_x, b[2, some(s + 1), at], 0.0)
+            up_y = jnp.where(y + 1 < GY * n_y, b[3, some(s), pl.ds(row + 1, 16)], 0.0)
             up_z = jnp.where(lane >= 128 - step, 0.0, roll(low_z, -step))
-            diagonal = SHIFT * b[1, s, pl.ds(row, 16)] + scale * (low_x + up_x + low_y + up_y + low_z + up_z)
+            diagonal = SHIFT * b[1, some(s), at] + scale * (low_x + up_x + low_y + up_y + low_z + up_z)
             inverse = jnp.where(ok, 1.0 / diagonal, 0.0)
             scaled = scale * inverse
-            c[1, s] = low_x * scaled
-            c[2, s] = up_x * scaled
-            c[3, s] = low_y * scaled
-            c[4, s] = up_y * scaled
-            c[5, s] = jnp.where(lane < step, 0.0, low_z * scaled)
-            c[6, s] = up_z * scaled
-            c[7, s] = diagonal
-            c[8, s] = inverse
+            c[1, some(s)] = low_x * scaled
+            c[2, some(s)] = up_x * scaled
+            c[3, some(s)] = low_y * scaled
+            c[4, some(s)] = up_y * scaled
+            c[5, some(s)] = jnp.where(lane < step, 0.0, low_z * scaled)
+            c[6, some(s)] = up_z * scaled
+            c[7, some(s)] = diagonal
+            c[8, some(s)] = inverse
 
         slots(lo, hi, body)
 
     def scaled_residual(c, w, v, s, step, rows=16, off=0):
         at = pl.ds(8 + off, rows)
-        centre = v[s + 1, at]
+        centre = v[some(s + 1), at]
         k = pl.ds(off, rows)
-        total = w[s, k] - centre
-        along_x = c[1, s, k] * v[s, at] + c[2, s, k] * v[s + 2, at]
-        along_y = c[3, s, k] * v[s + 1, pl.ds(7 + off, rows)] + c[4, s, k] * v[s + 1, pl.ds(9 + off, rows)]
-        along_z = c[5, s, k] * roll(centre, step) + c[6, s, k] * roll(centre, -step)
+        t = some(s)
+        total = w[t, k] - centre
+        along_x = c[1, t, k] * v[t, at] + c[2, t, k] * v[some(s + 2), at]
+        before, after = v[some(s + 1), pl.ds(7 + off, rows)], v[some(s + 1), pl.ds(9 + off, rows)]
+        along_y = c[3, t, k] * before + c[4, t, k] * after
+        along_z = c[5, t, k] * roll(centre, step) + c[6, t, k] * roll(centre, -step)
         return centre, total + (along_x + along_y) + along_z
 
     def sweep(c, w, v, a, s, step, k, first, rows=16, off=0):
@@ -305,46 +317,45 @@
         centre, r = scaled_residual(c, w, v[a], s, step, rows, off)
         change = gain * r
         if not first:
-            change = change + keep * (centre - v[1 - a][s + 1, pl.ds(8 + off, rows)])
+            change = change + keep * (centre - v[1 - a][some(s + 1), pl.ds(8 + off, rows)])
         return centre + change
 
     def smooth_up(b, c, w, v, row, step, lo, hi, rows, off):
         def begin(s):
-            g = b[0, s, pl.ds(row, 16)] * c[8, s]
-            w[s] = g
-            v[0][s + 1, pl.ds(8, 16)] = TABLE[0][1] * g
+            g = b[0, some(s), pl.ds(row, 16)] * c[8, some(s)]
+            w[some(s)] = g
+            v[0][some(s + 1), pl.ds(8, 16)] = TABLE[0][1] * g
 
         slots(lo, hi, begin)
 
         def second(s):
             keep, gain = TABLE[1]
             centre, r = scaled_residual(c, w, v[0], s, step)
-            v[1][s + 1, pl.ds(8, 16)] = centre + gain * r + keep * centre
+            v[1][some(s + 1), pl.ds(8, 16)] = centre + gain * r + keep * centre
 
         slots(lo + 1, hi - 1, second)
         for k in (2, 3):
             a = (k - 1) % 2
 
             def body(s, k=k, a=a):
-                v[1 - a][s + 1, pl.ds(8 + off, rows)] = sweep(c, w, v, a, s, step, k, False, rows, off)
+                v[1 - a][some(s + 1), pl.ds(8 + off, rows)] = sweep(c, w, v, a, s, step, k, False, rows, off)
 
             slots(lo + k, hi - k, body)
+
+    def pair_slots(value):
+        first, second = split_slots(value)
+        return first + second
 
     arrive(send_b0)
     prepare(b0, c0, 0, 1.0, 1, 16, 8, 4, 0, 24)
     smooth_up(b0, c0, w0, v0, 0, 1, 0, 24, 16, 0)
 
-    def resid0(i):
-        total = None
-        for j in range(2):
-            s = 4 + 2 * i + j
-            centre, r = scaled_residual(c0, w0, v0[1], s, 1, 8, 4)
-            x0[s, 4:12] = centre
-            r = r * c0[7, s, 4:12]
-            total = r if total is None else total + r
-        t0[i] = total
-
-    slots(0, 8, resid0)
+    def resid0(s):
+        centre, r = scaled_residual(c0, w0, v0[1], s, 1, 8, 4)
+        x0[some(s), 4:12] = centre
+        t0[pl.ds((s - 4) // 2, CHUNK // 2)] = pair_slots(r * c0[7, some(s), 4:12])
+
+    slots(4, 20, resid0)
     both = t0[:, pl.ds(0, 4, stride=2)] + t0[:, pl.ds(1, 4, stride=2)]
     f1 = pair_sum(both, 1) * 0.125
     b1[0, 8:16, 8:12] = f1
@@ -368,20 +379,15 @@
 
     smooth_up(b1, c1, w1, v1, 2, 2, 4, 20, 8, 4)
 
-    def resid1(i):
-        total = None
-        for j in range(2):
-            s = 8 + 2 * i + j
-            centre, r = scaled_residual(c1, w1, v1[1], s, 2, 4, 6)
-            x1[0, s, 8:12] = centre
-            r = r * c1[7, s, 6:10]
-            total = r if total is None else total + r
-        t1[i, 0:4] = total
-
-    slots(0, 4, resid1)
-    both = t1[:, pl.ds(0, 2, stride=2)] + t1[:, pl.ds(1, 2, stride=2)]
+    def resid1(s):
+        centre, r = scaled_residual(c1, w1, v1[1], s, 2, 4, 6)
+        x1[0, some(s), 8:12] = centre
+        t1[pl.ds((s - 8) // 2, CHUNK // 2), 0:4] = pair_slots(r * c1[7, some(s), 6:10])
+
+    slots(8, 16, resid1)
+    both = t1[0:4, pl.ds(0, 2, stride=2)] + t1[0:4, pl.ds(1, 2, stride=2)]
     g2[gx, own_rows(2)] = pack(pair_sum(both, 2) * 0.125)
-    send_r2a(lambda copy: copy.start())
+    start(send_r2a)
     start(send_x1)
 
     tile = (1, 8, 128)
@@ -542,7 +548,7 @@
                 for i in range(4):
                     a2[name, j, k, i] = turn[name, j, pl.ds(4 * k + i, 8, stride=16)]
     prepare_whole(a2, k2, 2)
-    send_r2a(lambda copy: copy.wait_recv())
+    arrive(send_r2a)
     start(send_r2b)
     coarsen_whole(a2, a3)
     prepare_whole(a3, k3, 3)
@@ -590,12 +596,18 @@
             pr[4 * block + x, pl.ds(0, 8, stride=2)] = one
             pr[4 * block + x, pl.ds(1, 8, stride=2)] = one
 
-    slots(0, 3, spread, 1)
+    for block in range(3):
+        spread(block)
+
+    def twice(value):
+        count = value.shape[0]
+        return jnp.broadcast_to(value[:, None], (count, 2, 16, 128)).reshape(2 * count, 16, 128)
 
     def correct1(s):
         ok, _, _ = valid(s, 2, 8, 8, 8, 4)
-        v1[0][s + 1, pl.ds(8, 16)] = jnp.where(ok, x1[0, s, pl.ds(2, 16)] + pr[s // 2], 0.0)
-        w1[s] = jnp.where(ok, x1[1, s, pl.ds(2, 16)] * c1[8, s], 0.0)
+        added = twice(pr[pl.ds(s // 2, CHUNK // 2)])
+        v1[0][some(s + 1), pl.ds(8, 16)] = jnp.where(ok, x1[0, some(s), pl.ds(2, 16)] + added, 0.0)
+        w1[some(s)] = jnp.where(ok, x1[1, some(s), pl.ds(2, 16)] * c1[8, some(s)], 0.0)
 
     slots(2, 22, correct1)
 
@@ -608,36 +620,34 @@
                     last(s, sweep(c, w, v, a, s, step, k, False, 8, 4))
                     return
                 value = sweep(c, w, v, a, s, step, k, k == 0)
-                v[1 - a][s + 1, pl.ds(8, 16)] = value
+                v[1 - a][some(s + 1), pl.ds(8, 16)] = value
 
             slots(lo + k, hi - k, body)
 
     def spread0(s, value):
-        t1[s - 6] = value
+        t1[some(s - 6)] = value
 
     smooth_down(c1, w1, v1, 2, 3, 21, spread0)
 
-    def widen(i):
-        pr[i, pl.ds(0, 8, stride=2)] = t1[i]
-        pr[i, pl.ds(1, 8, stride=2)] = t1[i]
-
-    slots(0, 12, widen)
+    for odd in range(2):
+        pr[:, pl.ds(odd, 8, stride=2)] = t1[...]
     arrive(send_x0)
 
     def correct0(s):
         ok, _, _ = valid(s, 0, 4, 16, 4, 8)
-        v0[0][s + 1, pl.ds(8, 16)] = jnp.where(ok, x0[s] + pr[s // 2], 0.0)
+        added = twice(pr[pl.ds(s // 2, CHUNK // 2)])
+        v0[0][some(s + 1), pl.ds(8, 16)] = jnp.where(ok, x0[some(s)] + added, 0.0)
 
     slots(0, 24, correct0)
 
     def finish(s, value):
-        out[s - 4] = value
+        out[some(s - 4)] = value
 
     smooth_down(c0, w0, v0, 1, 1, 23, finish)
 
-    for copy in send_b0 + send_c1 + send_f1 + send_x0 + send_x1 + send_r2b:
+    for copy in send_b0 + send_c1 + send_f1 + send_x0 + send_x1 + send_r2a + send_r2b:
         copy.wait_send()
-    for each in (send_c2a, send_c2b, send_c2c, send_r2a):
+    for each in (send_c2a, send_c2b, send_c2c):
         each(lambda copy: copy.wait_send())
 
 

time: 52 us -> 48.7 us (0.937)
  Pallas kernels: 50.4 us -> 47 us
    pallas_call x1, Pallas kernels: 50.4 us -> 47 us  [step(): pl.pallas_call(kernel, out_shape=jax.ShapeDtypeStruct((16, 8, 128), F32),...]
where the time goes in v4:
time: 48.7 us; the launch traced here: 48.5 us
  Pallas kernels  47 us (97%)
  local copies, waits for them, and re-layouts  1.47 us (3%)
    pallas_call x1, Pallas kernels, step(): pl.pallas_call(kernel, out_shape=jax.ShapeDtypeStruct((16, 8, 128), F32),...  47 us
    unnamed x1, local copies, waits for them, and re-layouts  1.47 us

profile of v4, /device:TPU:1, one launch (start us, length us, event | category | flops | bytes accessed | tf_op | source)
XLA Modules:
  0.0 48.5 jit_solution(2545068205301668493)
XLA Ops:
  0.0 47.0 %vcycle.1 = f32[16,8,128]{2,1,0:T(8,128)} custom-call(f32[16,8,128]{2,1,0:T(8,128)} %f_in.1, f32[16,8,128]{2,1,0:T(8,128)} %al_in.1, f32[16,8,128]{2,1,0:T(8,128)} %bx_in.1, f32[16,8,128]{2,1,0:T(8,128)} %by_in.1, f32[16,8,128]{2,1,0:T(8,128)} %bz_in.1), custom_call_target="tpu_custom_call" | custom-call | tf_op jit(solution)/shard_map/vcycle/pallas_call | solution.py:681
  47.0 1.5 %copy.7 = f32[16,8,128]{2,1,0:T(8,128)} copy(f32[16,8,128]{2,1,0:T(8,128)} %vcycle.1) | data formatting | bytes 131072

commit v5 on v4

--- a/solution.py
+++ b/solution.py
@@ -272,7 +272,7 @@
             body(first + CHUNK * i)
             return carry
 
-        lax.fori_loop(0, runs, run, 0, unroll=2)
+        lax.fori_loop(0, runs, run, 0, unroll=3)
 
     def some(s):
         return pl.ds(s, CHUNK)
@@ -365,16 +365,6 @@
 
     arrive(send_c1)
     prepare(b1, c1, 2, 0.25, 2, 8, 4, 8, 2, 22)
-
-    def forward(i, carry):
-        @pl.when(i > 1)
-        def _():
-            c2_gy(i - 1, c2b_base + i - 2).wait_recv()
-
-        c2_core(i, c2b_base + GY // 2 + i - 2).start()
-        return carry
-
-    lax.fori_loop(1, GY // 2 + 1, forward, 0)
     arrive(send_f1)
 
     smooth_up(b1, c1, w1, v1, 2, 2, 4, 20, 8, 4)
@@ -389,6 +379,17 @@
     g2[gx, own_rows(2)] = pack(pair_sum(both, 2) * 0.125)
     start(send_r2a)
     start(send_x1)
+
+    def forward(i, carry):
+        @pl.when(i > 1)
+        def _():
+            c2_gy(i - 1, c2b_base + i - 2).wait_recv()
+
+        c2_core(i, c2b_base + GY // 2 + i - 2).start()
+        return carry
+
+    lax.fori_loop(1, GY // 2 + 1, forward, 0)
+
 
     tile = (1, 8, 128)
     sub = lax.broadcasted_iota(jnp.int32, tile, 1)
@@ -680,7 +681,7 @@
             vmem += [(n, n, n, 8, 128)] * 3
     return pl.pallas_call(
         kernel,
-        out_shape=jax.ShapeDtypeStruct((16, 8, 128), F32),
+        out_shape=pltpu.VMEM((16, 8, 128), F32),
         in_specs=[pl.BlockSpec(memory_space=pl.ANY)] * 5,
         out_specs=pl.BlockSpec(memory_space=pltpu.VMEM),
         scratch_shapes=[pltpu.VMEM(shape, F32) for shape in vmem]

time: 48.7 us -> 45.7 us (0.938)
  Pallas kernels: 47 us -> 44.9 us
  local copies, waits for them, and re-layouts: 1.47 us -> 0.63 us
    pallas_call x1, Pallas kernels: 47 us -> 44.9 us  [step(): pl.pallas_call(kernel, out_shape=pltpu.VMEM((16, 8, 128), F32), in_specs=...]
    unnamed x1, local copies, waits for them, and re-layouts: 1.47 us -> 0.63 us
where the time goes in v5:
time: 45.7 us; the launch traced here: 45.5 us
  Pallas kernels  44.9 us (98%)
  local copies, waits for them, and re-layouts  0.63 us (1%)
    pallas_call x1, Pallas kernels, step(): pl.pallas_call(kernel, out_shape=pltpu.VMEM((16, 8, 128), F32), in_specs=...  44.9 us

profile of v5, /device:TPU:1, one launch (start us, length us, event | category | flops | bytes accessed | tf_op | source)
XLA Modules:
  0.0 45.5 jit_solution(11273197688314913921)
XLA Ops:
  0.0 44.9 %vcycle.1 = f32[16,8,128]{2,1,0:T(8,128)S(1)} custom-call(f32[16,8,128]{2,1,0:T(8,128)} %f_in.1, f32[16,8,128]{2,1,0:T(8,128)} %al_in.1, f32[16,8,128]{2,1,0:T(8,128)} %bx_in.1, f32[16,8,128]{2,1,0:T(8,128)} %by_in.1, f32[16,8,128]{2,1,0:T(8,128)} %bz_in.1), custom_call_target="tpu_custom_call" | custom-call | tf_op jit(solution)/shard_map/vcycle/pallas_call | solution.py:682
  44.9 0.6 %copy.7 = f32[16,8,128]{2,1,0:T(8,128)} copy(f32[16,8,128]{2,1,0:T(8,128)S(1)} %vcycle.1) | data formatting | bytes 131072

commit v6 on v5

--- a/solution.py
+++ b/solution.py
@@ -152,10 +152,17 @@
         counter[0] += 1
         return remote(g2.at[gx, own_rows(2)], g2.at[gx, own_rows(2)], counter[0] - 1, gx_peer(i))
 
-    send_b0 = halo(
-        lambda x, y: b0.at[:, x, y], NEAR, 4, 16, 4, 8,
-        lambda dx, dy: (5, 4, 5, 4) if dx == 0 or dy == 0 else (4, 4, 4, 4),
-    )
+    send_b0 = []
+    for dx, dy in NEAR[4:]:
+        for from_x, to_x, to_y in [(0, 1, 3), (1, 3, 2)] if dx > 0 and dy > 0 else [(0, 2, 4), (2, 4, 2)]:
+            lo_x = 4 + from_x if dx < 0 else 20 - to_x
+            lo_y = 4 if dy < 0 else 12 - to_y
+            w_x = to_x - from_x
+            src = b0.at[:, pl.ds(lo_x, w_x), pl.ds(lo_y, to_y)]
+            dst = b0.at[:, pl.ds(lo_x - 16 * dx, w_x), pl.ds(lo_y - 8 * dy, to_y)]
+            send_b0.append(remote(src, dst, counter[0], near(dx, dy)))
+            counter[0] += 1
+    send_b0 += halo(lambda x, y: b0.at[:, x, y], NEAR[:4], 4, 16, 4, 8, lambda dx, dy: (5, 4, 5, 4))
     send_c1 = halo(
         lambda x, y: b1.at[pl.ds(1, 4), x, y], NEAR + FAR_Y + FAR_XY, 8, 8, 8, 4,
         lambda dx, dy: (2, 2, 2, 1) if abs(dy) == 2 else (6, 5, 4, 4),
@@ -254,8 +261,6 @@
     start(send_b0)
     send_c2a(lambda copy: copy.start())
     start(send_c1)
-    send_c2a(lambda copy: copy.wait_recv())
-    send_c2b(lambda copy: copy.start())
 
     def valid(s, rows, off_x, n_x, off_y, n_y):
         shape = (CHUNK, 16, 128)
@@ -361,6 +366,8 @@
     b1[0, 8:16, 8:12] = f1
     x1[1, 8:16, 8:12] = f1
     start(send_f1)
+    send_c2a(lambda copy: copy.wait_recv())
+    send_c2b(lambda copy: copy.start())
     start(send_x0)
 
     arrive(send_c1)
@@ -653,7 +660,7 @@
 
 
 def step(right_side, alpha, beta_x, beta_y, beta_z):
-    copies = 8 + 14 + 8 + 8 + 14 + 2 * (GX - 1 + GY - 1)
+    copies = 12 + 14 + 8 + 8 + 14 + 2 * (GX - 1 + GY - 1)
     vmem = [
         (5, 25, 24, 128),
         (9, 24, 16, 128),

time: 45.7 us -> 44.5 us (0.974)
  Pallas kernels: 44.9 us -> 43.7 us
    pallas_call x1, Pallas kernels: 44.9 us -> 43.7 us  [step(): pl.pallas_call(kernel, out_shape=pltpu.VMEM((16, 8, 128), F32), in_specs=...]
where the time goes in v6:
time: 44.5 us; the launch traced here: 44.4 us
  Pallas kernels  43.7 us (98%)
  local copies, waits for them, and re-layouts  0.63 us (1%)
    pallas_call x1, Pallas kernels, step(): pl.pallas_call(kernel, out_shape=pltpu.VMEM((16, 8, 128), F32), in_specs=...  43.7 us

profile of v6, /device:TPU:1, one launch (start us, length us, event | category | flops | bytes accessed | tf_op | source)
XLA Modules:
  0.0 44.4 jit_solution(473189900256047481)
XLA Ops:
  0.0 43.7 %vcycle.1 = f32[16,8,128]{2,1,0:T(8,128)S(1)} custom-call(f32[16,8,128]{2,1,0:T(8,128)} %f_in.1, f32[16,8,128]{2,1,0:T(8,128)} %al_in.1, f32[16,8,128]{2,1,0:T(8,128)} %bx_in.1, f32[16,8,128]{2,1,0:T(8,128)} %by_in.1, f32[16,8,128]{2,1,0:T(8,128)} %bz_in.1), custom_call_target="tpu_custom_call" | custom-call | tf_op jit(solution)/shard_map/vcycle/pallas_call | solution.py:689
  43.8 0.6 %copy.7 = f32[16,8,128]{2,1,0:T(8,128)} copy(f32[16,8,128]{2,1,0:T(8,128)S(1)} %vcycle.1) | data formatting | bytes 131072

commit v7 on v6

--- a/solution.py
+++ b/solution.py
@@ -358,7 +358,7 @@
     def resid0(s):
         centre, r = scaled_residual(c0, w0, v0[1], s, 1, 8, 4)
         x0[some(s), 4:12] = centre
-        t0[pl.ds((s - 4) // 2, CHUNK // 2)] = pair_slots(r * c0[7, some(s), 4:12])
+        t0[pl.ds((s - 4) // 2, CHUNK // 2), 0:8] = pair_slots(r * c0[7, some(s), 4:12])
 
     slots(4, 20, resid0)
     both = t0[:, pl.ds(0, 4, stride=2)] + t0[:, pl.ds(1, 4, stride=2)]
@@ -633,12 +633,12 @@
             slots(lo + k, hi - k, body)
 
     def spread0(s, value):
-        t1[some(s - 6)] = value
+        t1[some(s - 6), 0:8] = value
 
     smooth_down(c1, w1, v1, 2, 3, 21, spread0)
 
     for odd in range(2):
-        pr[:, pl.ds(odd, 8, stride=2)] = t1[...]
+        pr[:, pl.ds(odd, 8, stride=2)] = t1[:, 0:8]
     arrive(send_x0)
 
     def correct0(s):
@@ -668,16 +668,16 @@
         (26, 32, 128),
         (26, 32, 128),
         (24, 16, 128),
-        (8, 8, 128),
+        (8, 16, 128),
         (5, 25, 24, 128),
         (9, 24, 16, 128),
         (24, 16, 128),
         (26, 32, 128),
         (26, 32, 128),
         (2, 24, 24, 128),
-        (12, 8, 128),
         (12, 16, 128),
-        (GX, 8 * GY, 128),
+        (12, 16, 128),
+        (GX, 8 * GY + 8, 128),
         (GX, 8 * GY, 128),
         (5, 4, 128, 128),
         (GX + 2, 80, 128),

time: 44.5 us -> 44.5 us (level)
  no operation moved by 1% of the time
where the time goes in v7:
time: 44.5 us; the launch traced here: 44.4 us
  Pallas kernels  43.7 us (98%)
  local copies, waits for them, and re-layouts  0.63 us (1%)
    pallas_call x1, Pallas kernels, step(): pl.pallas_call(kernel, out_shape=pltpu.VMEM((16, 8, 128), F32), in_specs=...  43.7 us

profile of v7, /device:TPU:1, one launch (start us, length us, event | category | flops | bytes accessed | tf_op | source)
XLA Modules:
  0.0 44.4 jit_solution(10691163818718623708)
XLA Ops:
  0.0 43.7 %vcycle.1 = f32[16,8,128]{2,1,0:T(8,128)S(1)} custom-call(f32[16,8,128]{2,1,0:T(8,128)} %f_in.1, f32[16,8,128]{2,1,0:T(8,128)} %al_in.1, f32[16,8,128]{2,1,0:T(8,128)} %bx_in.1, f32[16,8,128]{2,1,0:T(8,128)} %by_in.1, f32[16,8,128]{2,1,0:T(8,128)} %bz_in.1), custom_call_target="tpu_custom_call" | custom-call | tf_op jit(solution)/shard_map/vcycle/pallas_call | solution.py:689
  43.8 0.6 %copy.7 = f32[16,8,128]{2,1,0:T(8,128)} copy(f32[16,8,128]{2,1,0:T(8,128)S(1)} %vcycle.1) | data formatting | bytes 131072
